TPU v7x, 32 devices: a whole 2x2x4 slice. The times are simulated.
32 devices in a mesh: fsdp: 8 (over z, x), tp: 4 (over y, core).
Axes of the slice: x: 2, y: 2, z: 4, core: 2. Of those that a mesh axis runs over, the one named last changes fastest.
Arguments:
- layer_input: bfloat16 [32768, 768], P(('fsdp', 'tp')), may hold values from -6 to 6
- w_qkv: bfloat16 [768, 3, 768], P('fsdp', None, 'tp'), may hold values from -0.21875 to 0.21875
- bias_qv: bfloat16 [2, 768], P(None, 'tp'), may hold values from -3 to 3
- w_out: bfloat16 [768, 768], P('tp', 'fsdp'), may hold values from -0.875 to 0.875
- bias_out: bfloat16 [768], replicated, may hold values from -2 to 2
- gain_attn: bfloat16 [768], replicated, may hold values from 0.25 to 1.75
- shift_attn: bfloat16 [768], replicated, may hold values from -2 to 2
- gain_mlp: bfloat16 [768], replicated, may hold values from 0.25 to 1.75
- shift_mlp: bfloat16 [768], replicated, may hold values from -2 to 2
- w_up: bfloat16 [768, 3072], P('fsdp', 'tp'), may hold values from -0.21875 to 0.21875
- bias_up: bfloat16 [3072], P('tp'), may hold values from -3 to 3
- w_down: bfloat16 [3072, 768], P('tp', 'fsdp'), may hold values from -0.109375 to 0.109375
- bias_down: bfloat16 [768], replicated, may hold values from -2 to 2
- cotangent: bfloat16 [32768, 768], P(('fsdp', 'tp')), may hold values from -18 to 18
Outputs:
- layer_output: bfloat16 [32768, 768], P(('fsdp', 'tp'))
- grad_input: bfloat16 [32768, 768], P(('fsdp', 'tp'))
- grad_w_qkv: float32 [768, 3, 768], P('fsdp', None, 'tp')
- grad_bias_qv: float32 [2, 768], P(None, 'tp')
- grad_w_out: float32 [768, 768], P('tp', 'fsdp')
- grad_bias_out: float32 [768], replicated
- grad_gain_attn: float32 [768], replicated
- grad_shift_attn: float32 [768], replicated
- grad_gain_mlp: float32 [768], replicated
- grad_shift_mlp: float32 [768], replicated
- grad_w_up: float32 [768, 3072], P('fsdp', 'tp')
- grad_bias_up: float32 [3072], P('tp')
- grad_w_down: float32 [3072, 768], P('tp', 'fsdp')
- grad_bias_down: float32 [768], replicated
All inputs are finite; a program needn't handle non-finite values.
Results may differ from a plain program's by a relative error of at most 0.017.
Values may be sent and summed in bfloat16 or wider, within the bound.
No kernel may reach another device: no remote copies, remote signals or barrier semaphores. Data moves between devices by JAX's collectives and lax.ppermute only.
A program may use at most 192 MiB of HBM per device.

v0:
```python
import jax
import jax.numpy as jnp
from jax import lax
from jax.sharding import PartitionSpec as P

HEAD_DIM = 64
SEQ_LEN = 512


def normalize(rows, gain, shift):
    centre = rows - jnp.mean(rows, axis=-1, keepdims=True)
    spread = lax.rsqrt(jnp.mean(centre * centre, axis=-1, keepdims=True) + 1e-05)
    unit = centre * spread
    return (unit * gain.astype(jnp.float32) + shift.astype(jnp.float32), unit, spread)


def norm_back(grad_out, unit, spread, gain):
    scaled = grad_out * gain.astype(jnp.float32)
    inner = jnp.mean(scaled * unit, axis=-1, keepdims=True)
    return spread * (scaled - jnp.mean(scaled, axis=-1, keepdims=True) - unit * inner)


def gelu_exact(value):
    return 0.5 * value * (1.0 + lax.erf(value * 2.0 ** (-0.5)))


def gelu_slope(value):
    cumulative = 0.5 * (1.0 + lax.erf(value * 2.0 ** (-0.5)))
    density = jnp.exp(-0.5 * value * value) * (2.0 * 3.141592653589793) ** (-0.5)
    return cumulative + value * density


def contract_rows(left, right):
    return lax.dot_general(
        left, right, (((0,), (0,)), ((), ())), preferred_element_type=jnp.float32
    )


def against(left, right):
    return lax.dot_general(
        left, right, (((1,), (1,)), ((), ())), preferred_element_type=jnp.float32
    )


def fetch_attn(w_qkv, w_out, bias_qv):
    qkv_whole, out_whole = (
        lax.all_gather(w_qkv, "fsdp", axis=0, tiled=True),
        lax.all_gather(w_out, "fsdp", axis=1, tiled=True),
    )
    return (
        lax.all_gather(qkv_whole, "tp", axis=2, tiled=True),
        lax.all_gather(out_whole, "tp", axis=0, tiled=True),
        lax.all_gather(bias_qv, "tp", axis=1, tiled=True),
    )


def fetch_mlp(w_up, w_down, bias_up):
    up_whole, down_whole = (
        lax.all_gather(w_up, "fsdp", axis=0, tiled=True),
        lax.all_gather(w_down, "fsdp", axis=1, tiled=True),
    )
    return (
        lax.all_gather(up_whole, "tp", axis=1, tiled=True),
        lax.all_gather(down_whole, "tp", axis=0, tiled=True),
        lax.all_gather(bias_up, "tp", axis=0, tiled=True),
    )


def masked_scores(query, keys):
    scores = jnp.einsum(
        "sqhe,skhe->shqk", query, keys, preferred_element_type=jnp.float32
    ) * HEAD_DIM ** (-0.5)
    rows_idx = lax.broadcasted_iota(jnp.int32, (SEQ_LEN, SEQ_LEN), 0)
    cols_idx = lax.broadcasted_iota(jnp.int32, (SEQ_LEN, SEQ_LEN), 1)
    return jnp.where(rows_idx >= cols_idx, scores, -1e30)


def body(
    layer_input,
    w_qkv,
    bias_qv,
    w_out,
    bias_out,
    gain_attn,
    shift_attn,
    gain_mlp,
    shift_mlp,
    w_up,
    bias_up,
    w_down,
    bias_down,
    cotangent,
):
    resid = layer_input.astype(jnp.float32)
    normed_one, unit_one, spread_one = normalize(resid, gain_attn, shift_attn)
    rows_one = normed_one.astype(jnp.bfloat16)
    qkv_full, out_full, bias_qv_here = fetch_attn(w_qkv, w_out, bias_qv)
    bias_float = bias_qv_here.astype(jnp.float32)
    bias_three = jnp.stack([bias_float[0], jnp.zeros_like(bias_float[0]), bias_float[1]])
    projected = (
        jnp.einsum("td,dcf->tcf", rows_one, qkv_full, preferred_element_type=jnp.float32)
        + bias_three
    ).astype(jnp.bfloat16)
    group = rows_one.shape[0]
    seqs = group // SEQ_LEN
    width = projected.shape[2]
    heads_here = width // HEAD_DIM
    shaped = projected.reshape(seqs, SEQ_LEN, 3, heads_here, HEAD_DIM)
    query = shaped[:, :, 0]
    keys = shaped[:, :, 1]
    values = shaped[:, :, 2]
    scores = masked_scores(query, keys)
    top = jnp.max(scores, axis=-1, keepdims=True)
    log_total = top + jnp.log(jnp.sum(jnp.exp(scores - top), axis=-1, keepdims=True))
    probs = jnp.exp(scores - log_total).astype(jnp.bfloat16)
    mixed = (
        jnp.einsum("shqk,skhe->sqhe", probs, values, preferred_element_type=jnp.float32)
        .astype(jnp.bfloat16)
        .reshape(group, width)
    )
    attn_part = jnp.dot(mixed, out_full, preferred_element_type=jnp.float32)
    attended = attn_part + bias_out.astype(jnp.float32)
    middle = resid + attended
    normed_two, unit_two, spread_two = normalize(middle, gain_mlp, shift_mlp)
    rows_two = normed_two.astype(jnp.bfloat16)
    up_full, down_full, bias_up_here = fetch_mlp(w_up, w_down, bias_up)
    hidden_pre = jnp.dot(
        rows_two, up_full, preferred_element_type=jnp.float32
    ) + bias_up_here.astype(jnp.float32)
    hidden = gelu_exact(hidden_pre).astype(jnp.bfloat16)
    mlp_part = jnp.dot(hidden, down_full, preferred_element_type=jnp.float32)
    mlp_total = mlp_part + bias_down.astype(jnp.float32)
    layer_output = (middle + mlp_total).astype(jnp.bfloat16)
    up_back, down_back, unused_up = fetch_mlp(w_up, w_down, bias_up)
    qkv_back, out_back, unused_qv = fetch_attn(w_qkv, w_out, bias_qv)
    sum_down = jnp.sum(cotangent.astype(jnp.float32), axis=0)
    grad_down = contract_rows(hidden, cotangent)
    grad_hidden = against(cotangent, down_back)
    grad_pre = (grad_hidden * gelu_slope(hidden_pre)).astype(jnp.bfloat16)
    sum_up = jnp.sum(grad_pre.astype(jnp.float32), axis=0)
    grad_up = contract_rows(rows_two, grad_pre)
    grad_normed_two = against(grad_pre, up_back)
    grad_up, grad_down = (
        lax.psum_scatter(
            grad_up.astype(jnp.bfloat16), "tp", scatter_dimension=1, tiled=True
        ).astype(jnp.float32),
        lax.psum_scatter(
            grad_down.astype(jnp.bfloat16), "tp", scatter_dimension=0, tiled=True
        ).astype(jnp.float32),
    )
    shard_up, shard_down = (
        lax.psum_scatter(
            grad_up.astype(jnp.bfloat16), "fsdp", scatter_dimension=0, tiled=True
        ).astype(jnp.float32),
        lax.psum_scatter(
            grad_down.astype(jnp.bfloat16), "fsdp", scatter_dimension=1, tiled=True
        ).astype(jnp.float32),
    )
    gain_two_part = jnp.sum(grad_normed_two * unit_two, axis=0)
    shift_two_part = jnp.sum(grad_normed_two, axis=0)
    grad_middle = cotangent.astype(jnp.float32) + norm_back(
        grad_normed_two, unit_two, spread_two, gain_mlp
    )
    grad_rows = grad_middle.astype(jnp.bfloat16)
    sum_out = jnp.sum(grad_rows.astype(jnp.float32), axis=0)
    grad_wout = contract_rows(mixed, grad_rows)
    grad_mixed = (
        against(grad_rows, out_back)
        .astype(jnp.bfloat16)
        .reshape(seqs, SEQ_LEN, heads_here, HEAD_DIM)
    )
    again_scores = masked_scores(query, keys)
    probs_full = jnp.exp(again_scores - log_total)
    grad_probs = jnp.einsum(
        "sqhe,skhe->shqk", grad_mixed, values, preferred_element_type=jnp.float32
    )
    delta = jnp.sum(grad_probs * probs_full, axis=-1, keepdims=True)
    grad_scores = (probs_full * (grad_probs - delta)).astype(jnp.bfloat16)
    grad_values = jnp.einsum(
        "shqk,sqhe->skhe",
        probs_full.astype(jnp.bfloat16),
        grad_mixed,
        preferred_element_type=jnp.float32,
    )
    grad_query = jnp.einsum(
        "shqk,skhe->sqhe", grad_scores, keys, preferred_element_type=jnp.float32
    ) * HEAD_DIM ** (-0.5)
    grad_keys = jnp.einsum(
        "shqk,sqhe->skhe", grad_scores, query, preferred_element_type=jnp.float32
    ) * HEAD_DIM ** (-0.5)
    grad_proj = (
        jnp.stack([grad_query, grad_keys, grad_values], axis=2)
        .astype(jnp.bfloat16)
        .reshape(group, 3, width)
    )
    sum_three = jnp.sum(grad_proj.astype(jnp.float32), axis=0)
    sum_qv = jnp.stack([sum_three[0], sum_three[2]])
    grad_wqkv = jnp.einsum("td,tcf->dcf", rows_one, grad_proj, preferred_element_type=jnp.float32)
    grad_normed_one = jnp.einsum(
        "tcf,dcf->td", grad_proj, qkv_back, preferred_element_type=jnp.float32
    )
    grad_wqkv, grad_wout = (
        lax.psum_scatter(
            grad_wqkv.astype(jnp.bfloat16), "tp", scatter_dimension=2, tiled=True
        ).astype(jnp.float32),
        lax.psum_scatter(
            grad_wout.astype(jnp.bfloat16), "tp", scatter_dimension=0, tiled=True
        ).astype(jnp.float32),
    )
    shard_qkv, shard_out = (
        lax.psum_scatter(
            grad_wqkv.astype(jnp.bfloat16), "fsdp", scatter_dimension=0, tiled=True
        ).astype(jnp.float32),
        lax.psum_scatter(
            grad_wout.astype(jnp.bfloat16), "fsdp", scatter_dimension=1, tiled=True
        ).astype(jnp.float32),
    )
    gain_one_part = jnp.sum(grad_normed_one * unit_one, axis=0)
    shift_one_part = jnp.sum(grad_normed_one, axis=0)
    grad_input = (grad_middle + norm_back(grad_normed_one, unit_one, spread_one, gain_attn)).astype(
        jnp.bfloat16
    )
    sum_qv, sum_up, sum_out, sum_down = lax.psum((sum_qv, sum_up, sum_out, sum_down), "tp")
    parts = lax.axis_size("tp")
    place = lax.axis_index("tp")
    qv_width = sum_qv.shape[1] // parts
    up_width = sum_up.shape[0] // parts
    sum_qv = lax.dynamic_slice_in_dim(sum_qv, place * qv_width, qv_width, 1)
    sum_up = lax.dynamic_slice_in_dim(sum_up, place * up_width, up_width, 0)
    total_qv, total_up, total_out, total_down = lax.psum(
        (sum_qv, sum_up, sum_out, sum_down), "fsdp"
    )
    gain_one, shift_one, gain_two, shift_two = lax.psum(
        (gain_one_part, shift_one_part, gain_two_part, shift_two_part), ("fsdp", "tp")
    )
    return (
        layer_output,
        grad_input,
        shard_qkv,
        total_qv,
        shard_out,
        total_out,
        gain_one,
        shift_one,
        gain_two,
        shift_two,
        shard_up,
        total_up,
        shard_down,
        total_down,
    )


def solution(mesh):
    placed = (
        P(("fsdp", "tp"), None),
        P("fsdp", None, "tp"),
        P(None, "tp"),
        P("tp", "fsdp"),
        P(),
        P(),
        P(),
        P(),
        P(),
        P("fsdp", "tp"),
        P("tp"),
        P("tp", "fsdp"),
        P(),
        P(("fsdp", "tp"), None),
    )
    return jax.shard_map(
        body,
        mesh=mesh,
        in_specs=placed,
        out_specs=(
            P(("fsdp", "tp"), None),
            P(("fsdp", "tp"), None),
            P("fsdp", None, "tp"),
            P(None, "tp"),
            P("tp", "fsdp"),
            P(),
            P(),
            P(),
            P(),
            P(),
            P("fsdp", "tp"),
            P("tp"),
            P("tp", "fsdp"),
            P(),
        ),
        check_vma=False,
    )
```

profile of v0, /device:TPU:0, one launch (start us, length us, event | category | flops | bytes accessed | tf_op | source)
XLA Modules:
  0.0 791.1 jit_solution(17677742210459713364)
XLA Ops:
  9.8 42.0 %all_gather.38 = bf16[768,3,192]{2,1,0:T(4,128)(2,1)S(1)} all-gather(bf16[96,3,192]{2,1,0:T(4,128)(2,1)S(1)} %copy.160), channel_id=1, replica_groups=mesh['fsdp'=8,'tp'=4] {'fsdp'}, dimensions={0}, use_global_device_ids=true | all-gather | bytes 995328 | tf_op jit(solution)/shard_map/all_gather | solution.py:47
  54.0 31.8 %all_gather.41 = bf16[192,768]{0,1:T(8,128)(2,1)S(1)} all-gather(bf16[192,96]{0,1:T(8,128)(2,1)S(1)} %copy.170), channel_id=1, replica_groups=mesh['fsdp'=8,'tp'=4] {'fsdp'}, dimensions={1}, use_global_device_ids=true | all-gather | bytes 331776 | tf_op jit(solution)/shard_map/all_gather | solution.py:48
  92.6 5.2 all-gather.1
  105.1 31.1 %all-gather.9.cloned.1.call-done = bf16[768,3,768]{0,2,1:T(8,128)(2,1)} async-done(((bf16[768,3,192]{0,2,1:T(8,128)(2,1)}), bf16[768,3,768]{0,2,1:T(8,128)(2,1)}) %all-gather.9.cloned.1.call-update) | async-done | bytes 3538960 | tf_op jit(solution)/shard_map/all_gather | solution.py:51
  136.2 8.0 %add_convert_fusion = bf16[1024,3,768]{2,0,1:T(8,128)(2,1)} fusion(f32[3,768]{1,0:T(4,128)S(1)} %pad_maximum_fusion.1, bf16[768,3,768]{0,2,1:T(8,128)(2,1)} %all-gather.9.cloned.1.call-done, bf16[1024,768]{0,1:T(8,128)(2,1)S(1)} %copy.159, f32[768]{0:T(1024)S(1)} %convert_element_type.118, f32[768]{0:T(1024)S(1)} %convert_element_type.117, ...), kind=kOutput, calls=%fused_computation.18 | convolution fusion | flops 3633315840 | bytes 9853952 | tf_op jit(solution)/shard_map/td,dcf->tcf/dot_general | solution.py:101
  144.3 6.6 copy.164
  150.9 8.8 %reshape.105 = bf16[2,512,3,12,64]{1,0,4,3,2:T(2,128)(2,1)} reshape(bf16[1024,3,768]{0,2,1:T(8,128)(2,1)} %copy.164) | data formatting | bytes 9437184 | tf_op jit(solution)/shard_map/reshape | solution.py:108
  164.8 10.5 %fusion = (f32[2,12,512]{2,1,0:T(8,128)S(1)}, f32[2,12,512,512]{2,3,1,0:T(8,128)}) fusion(pred[512,512]{0,1:T(8,128)(4,1)S(1)} %iota_compare_fusion, bf16[2,512,1,12,64]{1,0,4,3,2:T(2,128)(2,1)S(1)} %get-tuple-element.104, bf16[2,512,1,12,64]{1,0,4,3,2:T(2,128)(2,1)S(1)} %get-tuple-element.105), kind=kOutput, calls=%fused_computation.5 | convolution fusion | flops 824168448 | bytes 28622848 | tf_op jit(solution)/shard_map/sqhe,skhe->shqk/dot_general | solution.py:70
  175.4 11.2 %exponential_reduce_fusion = f32[2,12,512]{2,1,0:T(8,128)S(1)} fusion(f32[2,12,512,512]{2,3,1,0:T(8,128)} %get-tuple-element.113, f32[2,12,512]{2,1,0:T(8,128)S(1)} %get-tuple-element.112, pred[512,512]{0,1:T(8,128)(4,1)S(1)} %iota_compare_fusion), kind=kLoop, calls=%fused_computation.3 | loop fusion | flops 25153536 | bytes 25526272 | tf_op jit(solution)/shard_map/reduce_sum | solution.py:114
  186.6 11.7 %fusion.24 = bf16[2,512,12,64]{1,3,2,0:T(8,128)(2,1)S(1)} fusion(bf16[2,512,1,12,64]{1,0,4,3,2:T(2,128)(2,1)S(1)} %get-tuple-element.106, f32[2,12,512,512]{2,3,1,0:T(8,128)} %get-tuple-element.113, f32[2,12,512]{2,1,0:T(8,128)S(1)} %log_add_fusion, pred[512,512]{0,1:T(8,128)(4,1)S(1)} %iota_compare_fusion), kind=kOutput, calls=%fused_computation.63 | convolution fusion | flops 831258624 | bytes 28622848 | tf_op jit(solution)/shard_map/shqk,skhe->sqhe/dot_general | solution.py:117
  207.2 13.7 %multiply_convert_fusion.1 = (bf16[1024,3072]{1,0:T(8,128)(2,1)}, f32[1024,3072]{1,0:T(8,128)}) fusion(f32[3072]{0:T(1024)S(1)} %bitcast.91, bf16[768,3072]{1,0:T(8,128)(2,1)} %all-gather.15.cloned.1.call-done, f32[1024,768]{0,1:T(8,128)} %copy-done.1, f32[768]{0:T(1024)S(1)} %convert_element_type.127, f32[768]{0:T(1024)S(1)} %convert_element_type.126, ...), kind=kOutput, calls=%fused_computation.15 | convolution fusion | flops 4854644736 | bytes 26765312 | tf_op jit(solution)/shard_map/dot_general | solution.py:127
  220.9 12.6 %all-gather.19.cloned.1.call-done = bf16[3072,768]{0,1:T(8,128)(2,1)} async-done(((bf16[768,768]{0,1:T(8,128)(2,1)}), bf16[3072,768]{0,1:T(8,128)(2,1)}) %all-gather.19.cloned.1.call-update) | async-done | bytes 4718608 | tf_op jit(solution)/shard_map/all_gather | solution.py:64
  233.5 13.1 %convert_reduce_fusion = (f32[3072]{0:T(1024)}, bf16[1024,3072]{1,0:T(8,128)(2,1)S(1)}) fusion(f32[1024,3072]{1,0:T(8,128)} %get-tuple-element.117, f32[3072]{0:T(1024)S(1)} %bitcast.92, bf16[1024,768]{1,0:T(8,128)(2,1)} %param.27, bf16[3072,768]{0,1:T(8,128)(2,1)} %all-gather.19.cloned.1.call-done), kind=kOutput, calls=%fused_computation.14 | convolution fusion | flops 4872729600 | bytes 25190400 | tf_op jit(solution)/shard_map/dot_general | solution.py:40
  246.6 7.4 fusion.48
  281.6 12.9 %fusion.25 = bf16[2,512,12,64]{1,3,2,0:T(8,128)(2,1)} fusion(bf16[2,512,12,64]{1,0,3,2:T(2,128)(2,1)} %reshape.107, f32[2,12,512,512]{2,3,1,0:T(8,128)} %get-tuple-element.113, f32[2,12,512]{2,1,0:T(8,128)S(1)} %log_add_fusion, pred[512,512]{0,1:T(8,128)(4,1)S(1)} %iota_compare_fusion), kind=kOutput, calls=%fused_computation.64 | convolution fusion | flops 831258624 | bytes 28622848 | tf_op jit(solution)/shard_map/shqk,sqhe->skhe/dot_general | solution.py:179
  294.6 17.4 %multiply_reduce_fusion = (f32[2,12,512]{2,1,0:T(8,128)S(1)}, f32[2,12,512,512]{2,3,1,0:T(8,128)}) fusion(f32[2,12,512,512]{2,3,1,0:T(8,128)} %get-tuple-element.113, f32[2,12,512]{2,1,0:T(8,128)S(1)} %log_add_fusion, pred[512,512]{0,1:T(8,128)(4,1)S(1)} %iota_compare_fusion, bf16[2,512,1,12,64]{1,0,4,3,2:T(2,128)(2,1)} %copy-done.8, ...), kind=kOutput, calls=%fused_computation.1 | convolution fusion | flops 836751360 | bytes 53837824 | tf_op jit(solution)/shard_map/sqhe,skhe->shqk/dot_general | solution.py:174
  322.8 17.3 %multiply_convert_fusion = bf16[2,12,512,512]{2,3,1,0:T(8,128)(2,1)S(1)} fusion(f32[2,12,512,512]{2,3,1,0:T(8,128)} %get-tuple-element.119, f32[2,12,512,512]{2,3,1,0:T(8,128)} %get-tuple-element.113, f32[2,12,512]{2,1,0:T(8,128)S(1)} %get-tuple-element.118, f32[2,12,512]{2,1,0:T(8,128)S(1)} %log_add_fusion, pred[512,512]{0,1:T(8,128)(4,1)S(1)} %iota_compare_fusion), kind=kLoop, calls=%fused_computation | loop fusion | flops 37748736 | bytes 63275008 | tf_op jit(solution)/shard_map/convert_element_type | solution.py:178
  353.9 8.5 %fusion.27 = bf16[2,512,12,64]{1,3,2,0:T(8,128)(2,1)S(1)} fusion(bf16[2,12,512,512]{2,3,1,0:T(8,128)(2,1)} %copy-done, bf16[2,512,1,12,64]{1,0,4,3,2:T(2,128)(2,1)S(1)} %copy-done.6), kind=kOutput, calls=%fused_computation.66 | convolution fusion | flops 806879232 | bytes 15728640 | tf_op jit(solution)/shard_map/shqk,sqhe->skhe/dot_general | solution.py:188
  369.4 7.8 convolution_convert_fusion.2
  377.3 9.2 %convolution_convert_fusion = bf16[3072,768]{1,0:T(8,128)(2,1)} fusion(bf16[1024,3072]{1,0:T(8,128)(2,1)} %get-tuple-element.116, bf16[1024,768]{1,0:T(8,128)(2,1)} %param.27), kind=kOutput, calls=%fused_computation.19 | convolution fusion | flops 4834197504 | bytes 12582912 | tf_op jit(solution)/shard_map/dot_general | solution.py:34
  387.2 10.0 %convolution_convert_fusion.1 = bf16[768,3072]{1,0:T(8,128)(2,1)} fusion(bf16[1024,3072]{1,0:T(8,128)(2,1)} %copy-done.37, f32[1024,768]{0,1:T(8,128)} %copy-done.1, f32[768]{0:T(1024)S(1)} %copy-done.24, f32[768]{0:T(1024)S(1)} %convert_element_type.126, f32[1024]{0:T(1024)S(1)} %add_rsqrt_fusion, f32[1024]{0:T(1024)S(1)} %broadcast_multiply_fusion.4), kind=kOutput, calls=%fused_computation.20 | convolution fusion | flops 4838129664 | bytes 14170112 | tf_op jit(solution)/shard_map/dot_general | solution.py:34
  399.2 18.8 %reduce-scatter.15.cloned.1.call-done = bf16[768,3,192]{0,2,1:T(8,128)(2,1)} async-done(((bf16[768,3,768]{0,2,1:T(8,128)(2,1)}), bf16[768,3,192]{0,2,1:T(8,128)(2,1)}) %reduce-scatter.15.cloned.1.call-update) | async-done | bytes 884752 | tf_op jit(solution)/shard_map/reduce_scatter | solution.py:203
  420.3 48.1 %reduce-scatter.23.cloned.1.call-done = bf16[768,768]{1,0:T(8,128)(2,1)} async-done(((bf16[3072,768]{1,0:T(8,128)(2,1)}), bf16[768,768]{1,0:T(8,128)(2,1)}) %reduce-scatter.23.cloned.1.call-update) | async-done | bytes 1179664 | tf_op jit(solution)/shard_map/reduce_scatter | solution.py:147
  470.9 10.2 %add_convert_fusion.1 = bf16[1024,768]{0,1:T(8,128)(2,1)} fusion(f32[1024,768]{0,1:T(8,128)} %copy-done.1, bf16[1024,3072]{1,0:T(8,128)(2,1)} %get-tuple-element.116, bf16[3072,768]{0,1:T(8,128)(2,1)} %all-gather.19.cloned.1.call-done, f32[768]{0:T(1024)S(1)} %convert_element_type.131), kind=kOutput, calls=%fused_computation.47 | convolution fusion | flops 4834197504 | bytes 15731712 | tf_op jit(solution)/shard_map/dot_general | solution.py:131
  481.1 37.7 %reduce-scatter.19.cloned.1.call-done = bf16[768,768]{1,0:T(8,128)(2,1)} async-done(((bf16[768,3072]{1,0:T(8,128)(2,1)}), bf16[768,768]{1,0:T(8,128)(2,1)}) %reduce-scatter.19.cloned.1.call-update) | async-done | bytes 1179664 | tf_op jit(solution)/shard_map/reduce_scatter | solution.py:144
  518.8 8.4 %fusion.47 = (f32[768]{0:T(1024)S(1)}, f32[1024,768]{1,0:T(8,128)}) fusion(bf16[768,3,768]{0,2,1:T(8,128)(2,1)} %all-gather.9.cloned.1.call-done, bf16[1024,1,768]{2,0,1:T(8,128)(2,1)S(1)} %copy-done.9, bf16[1024,1,768]{2,0,1:T(8,128)(2,1)} %copy.185, bf16[1024,1,768]{2,0,1:T(8,128)(2,1)} %copy.184), kind=kOutput, calls=%fused_computation.96 | convolution fusion | flops 3629382912 | bytes 11406336 | tf_op jit(solution)/shard_map/tcf,dcf->td/dot_general | solution.py:199
  545.3 10.7 %all-reduce.2 = (f32[2,768]{1,0:T(2,128)S(1)}, f32[768]{0:T(1024)S(1)}, f32[3072]{0:T(1024)S(1)}, f32[768]{0:T(1024)S(1)}) all-reduce(f32[2,768]{1,0:T(2,128)S(1)} %pad_maximum_fusion.2, f32[768]{0:T(1024)S(1)} %copy-done.20, f32[3072]{0:T(1024)S(1)} %copy-done.22, f32[768]{0:T(1024)S(1)} %copy-done.21), channel_id=1, replica_groups=mesh['fsdp'=8,'tp'=4] {'tp'}, use_global_device_ids=true, to_apply=%region_14.15 | all-reduce | flops 6144 | bytes 49152 | tf_op jit(solution)/shard_map/psum | solution.py:223
  556.2 37.6 %all-reduce.1 = (f32[2,192]{1,0:T(2,128)}, f32[768]{0:T(1024)}, f32[768]{0:T(1024)}, f32[768]{0:T(1024)}) all-reduce(f32[2,192]{1,0:T(2,128)S(1)} %constant_dynamic-slice_fusion, f32[768]{0:T(1024)S(1)} %get-tuple-element.99, f32[768]{0:T(1024)S(1)} %dynamic_slice.7, ...), channel_id=1, replica_groups=mesh['fsdp'=8,'tp'=4] {'fsdp'}, use_global_device_ids=true, to_apply=%region_15.16 | all-reduce | flops 2688 | bytes 21504 | tf_op jit(solution)/shard_map/psum | solution.py:230
  593.8 37.5 %all-reduce = (f32[768]{0:T(1024)}, f32[768]{0:T(1024)}, f32[768]{0:T(1024)}, f32[768]{0:T(1024)}) all-reduce(f32[768]{0:T(1024)S(1)} %get-tuple-element.86, f32[768]{0:T(1024)S(1)} %get-tuple-element.122, f32[768]{0:T(1024)S(1)} %get-tuple-element.84, f32[768]{0:T(1024)S(1)} %copy-done.27), channel_id=1, replica_groups=mesh['fsdp'=8,'tp'=4] {'fsdp','tp'}, use_global_device_ids=true, to_apply=%region_22.23 | all-reduce | flops 3072 | bytes 24576 | tf_op jit(solution)/shard_map/psum | solution.py:233
  632.8 16.4 %reduce-scatter.25.cloned.1.call-done = bf16[96,576]{1,0:T(8,128)(2,1)} async-done(((bf16[768,576]{1,0:T(8,128)(2,1)}), bf16[96,576]{1,0:T(8,128)(2,1)}) %reduce-scatter.25.cloned.1.call-update) | async-done | bytes 110608
  651.1 64.9 %reduce-scatter.29.cloned.1.call-done = bf16[96,768]{1,0:T(8,128)(2,1)} async-done(((bf16[768,768]{1,0:T(8,128)(2,1)}), bf16[96,768]{1,0:T(8,128)(2,1)}) %reduce-scatter.29.cloned.1.call-update) | async-done | bytes 147472
  718.0 64.7 %reduce-scatter.21.cloned.1.call-done = bf16[96,768]{1,0:T(8,128)(2,1)} async-done(((bf16[768,768]{1,0:T(8,128)(2,1)}), bf16[96,768]{1,0:T(8,128)(2,1)}) %reduce-scatter.21.cloned.1.call-update) | async-done | bytes 147472 | tf_op jit(solution)/shard_map/reduce_scatter | solution.py:152
  (183 shorter events, 124.4 us)
Async XLA Ops:
  7.2 46.7 %copy-start.15 = (bf16[192,96]{1,0:T(8,128)(2,1)S(1)}, bf16[192,96]{1,0:T(8,128)(2,1)}, u32[]{:S(2)}) copy-start(bf16[192,96]{1,0:T(8,128)(2,1)} %param.17) | copy-start | bytes 110596
  7.2 79.5 %all-gather.13.cloned.1.call-start = ((), (), s32[]{:S(2)}) async-start(), calls=%async_computation.10 | async-start | bytes 1327104 | tf_op jit(solution)/shard_map/all_gather | solution.py:59
  7.9 96.6 %all-gather.17.cloned.1.call-start = ((), (), s32[]{:S(2)}) async-start(), calls=%async_computation.12 | async-start | bytes 1327104 | tf_op jit(solution)/shard_map/all_gather | solution.py:60
  8.7 127.5 %all-gather.9.cloned.1.call-start = ((), (), s32[]{:S(2)}) async-start(), calls=%async_computation.8 | async-start | bytes 4423680 | tf_op jit(solution)/shard_map/all_gather | solution.py:51
  51.8 35.5 %copy-start.34 = (bf16[768]{0:T(1024)(128)(2,1)S(1)}, bf16[768]{0:T(1024)(128)(2,1)}, u32[]{:S(2)}) copy-start(bf16[768]{0:T(1024)(128)(2,1)} %param.24) | copy-start | bytes 4612
  51.8 35.6 %copy-start.28 = (bf16[768]{0:T(1024)(128)(2,1)S(1)}, bf16[768]{0:T(1024)(128)(2,1)}, u32[]{:S(2)}) copy-start(bf16[768]{0:T(1024)(128)(2,1)} %param.19) | copy-start | bytes 4612
  51.8 35.6 %copy-start.29 = (bf16[768]{0:T(1024)(128)(2,1)S(1)}, bf16[768]{0:T(1024)(128)(2,1)}, u32[]{:S(2)}) copy-start(bf16[768]{0:T(1024)(128)(2,1)} %param.21) | copy-start | bytes 4612
  51.8 35.6 %copy-start.30 = (bf16[768]{0:T(1024)(128)(2,1)S(1)}, bf16[768]{0:T(1024)(128)(2,1)}, u32[]{:S(2)}) copy-start(bf16[768]{0:T(1024)(128)(2,1)} %param.20) | copy-start | bytes 4612
  51.8 35.6 %copy-start.31 = (bf16[768]{0:T(1024)(128)(2,1)S(1)}, bf16[768]{0:T(1024)(128)(2,1)}, u32[]{:S(2)}) copy-start(bf16[768]{0:T(1024)(128)(2,1)} %param.22) | copy-start | bytes 4612
  51.8 35.7 %copy-start.35 = (bf16[2,192]{1,0:T(2,128)(2,1)S(1)}, bf16[2,192]{1,0:T(2,128)(2,1)}, u32[]{:S(2)}) copy-start(bf16[2,192]{1,0:T(2,128)(2,1)} %param.16) | copy-start | bytes 2308
  51.8 40.8 %copy-start.32 = (bf16[768]{0:T(1024)(128)(2,1)S(1)}, bf16[768]{0:T(1024)(128)(2,1)}, u32[]{:S(2)}) copy-start(bf16[768]{0:T(1024)(128)(2,1)} %param.18) | copy-start | bytes 4612
  51.8 46.0 %copy-start.11 = (bf16[1024,768]{1,0:T(8,128)(2,1)S(1)}, bf16[1024,768]{1,0:T(8,128)(2,1)}, u32[]{:S(2)}) copy-start(bf16[1024,768]{1,0:T(8,128)(2,1)} %param.14) | copy-start | bytes 4718596
  53.9 147.6 %all-gather.11.cloned.1.call-start = ((), (), s32[]{:S(2)}) async-start(), calls=%async_computation.9 | async-start | bytes 1474560 | tf_op jit(solution)/shard_map/all_gather | solution.py:52
  86.7 120.5 %all-gather.15.cloned.1.call-start = ((), (), s32[]{:S(2)}) async-start(), calls=%async_computation.11 | async-start | bytes 5898240 | tf_op jit(solution)/shard_map/all_gather | solution.py:63
  87.3 146.3 %all-gather.19.cloned.1.call-start = ((), (), s32[]{:S(2)}) async-start(), calls=%async_computation.13 | async-start | bytes 5898240 | tf_op jit(solution)/shard_map/all_gather | solution.py:64
  87.4 48.9 %copy-start.16 = (f32[768]{0:T(1024)}, f32[768]{0:T(1024)S(1)}, u32[]{:S(2)}) copy-start(f32[768]{0:T(1024)S(1)} %convert_element_type.117) | copy-start | bytes 9220
  87.4 48.8 %copy-start.25 = (f32[768]{0:T(1024)}, f32[768]{0:T(1024)S(1)}, u32[]{:S(2)}) copy-start(f32[768]{0:T(1024)S(1)} %convert_element_type.118) | copy-start | bytes 9220
  87.4 119.8 %copy-start.23 = (f32[768]{0:T(1024)}, f32[768]{0:T(1024)S(1)}, u32[]{:S(2)}) copy-start(f32[768]{0:T(1024)S(1)} %convert_element_type.127) | copy-start | bytes 9220
  101.6 42.7 %copy-start.13 = (f32[1024]{0:T(1024)}, f32[1024]{0:T(1024)S(1)}, u32[]{:S(2)}) copy-start(f32[1024]{0:T(1024)S(1)} %broadcast_multiply_fusion.5) | copy-start | bytes 12292
  102.1 42.2 %copy-start.18 = (f32[1024]{0:T(1024)}, f32[1024]{0:T(1024)S(1)}, u32[]{:S(2)}) copy-start(f32[1024]{0:T(1024)S(1)} %add_rsqrt_fusion.1) | copy-start | bytes 12292
  104.5 292.7 %reduce-scatter.17.cloned.1.call-start = ((), (), s32[]{:S(2)}) async-start(), calls=%async_computation.15 | async-start | bytes 1474560 | tf_op jit(solution)/shard_map/reduce_scatter | solution.py:206
  164.8 21.7 %copy-start.8 = (bf16[2,512,1,12,64]{1,0,4,3,2:T(2,128)(2,1)}, bf16[2,512,1,12,64]{1,0,4,3,2:T(2,128)(2,1)S(1)}, u32[]{:S(2)}) copy-start(bf16[2,512,1,12,64]{1,0,4,3,2:T(2,128)(2,1)S(1)} %get-tuple-element.106) | copy-start | bytes 4718596
  233.5 13.1 %copy-start.36 = (bf16[768,3072]{1,0:T(8,128)(2,1)S(1)}, bf16[768,3072]{1,0:T(8,128)(2,1)}, u32[]{:S(2)}) copy-start(bf16[768,3072]{1,0:T(8,128)(2,1)} %all-gather.15.cloned.1.call-done) | copy-start | bytes 14155780
  312.0 106.0 %reduce-scatter.15.cloned.1.call-start = ((), (), s32[]{:S(2)}) async-start(), calls=%async_computation.14 | async-start | bytes 4423680 | tf_op jit(solution)/shard_map/reduce_scatter | solution.py:203
  377.3 91.1 %reduce-scatter.23.cloned.1.call-start = ((), (), s32[]{:S(2)}) async-start(), calls=%async_computation.18 | async-start | bytes 5898240 | tf_op jit(solution)/shard_map/reduce_scatter | solution.py:147
  386.5 132.3 %reduce-scatter.19.cloned.1.call-start = ((), (), s32[]{:S(2)}) async-start(), calls=%async_computation.16 | async-start | bytes 5898240 | tf_op jit(solution)/shard_map/reduce_scatter | solution.py:144
  397.2 234.0 %reduce-scatter.27.cloned.1.call-start = ((), (), s32[]{:S(2)}) async-start(), calls=%async_computation.20 | async-start | bytes 442368
  399.2 250.0 %reduce-scatter.25.cloned.1.call-start = ((), (), s32[]{:S(2)}) async-start(), calls=%async_computation.19 | async-start | bytes 1105920
  418.0 52.9 %copy-start.33 = (bf16[768]{0:T(1024)(128)(2,1)S(1)}, bf16[768]{0:T(1024)(128)(2,1)}, u32[]{:S(2)}) copy-start(bf16[768]{0:T(1024)(128)(2,1)} %param.26) | copy-start | bytes 4612
  420.2 295.8 %reduce-scatter.29.cloned.1.call-start = ((), (), s32[]{:S(2)}) async-start(), calls=%async_computation.21 | async-start | bytes 1327104
  470.8 311.8 %reduce-scatter.21.cloned.1.call-start = ((), (), s32[]{:S(2)}) async-start(), calls=%async_computation.17 | async-start | bytes 1327104 | tf_op jit(solution)/shard_map/reduce_scatter | solution.py:152
  543.3 50.4 %copy-start.27 = (f32[768]{0:T(1024)S(1)}, f32[768]{0:T(1024)}, u32[]{:S(2)}) copy-start(f32[768]{0:T(1024)} %get-tuple-element.124) | copy-start | bytes 9220
  (20 other events, 83.1 us)
Sparse Core Ops, SparseCore 0:
  10.2 50.5 all-gather.12
  63.0 41.4 all-gather.16
  106.6 29.5 all-gather.8
  138.2 17.4 all-gather.10
  157.1 37.4 all-gather.14
  196.0 37.4 all-gather.18
  312.1 25.7 reduce-scatter.16
  377.4 40.5 reduce-scatter.14
  420.5 47.8 reduce-scatter.22
  470.9 47.8 reduce-scatter.18
  522.1 61.3 reduce-scatter.26
  586.7 62.4 reduce-scatter.24
  652.9 63.0 reduce-scatter.28
  719.6 63.0 reduce-scatter.20
where the time goes:
time: 796 us; the launch traced here: 791 us
  waiting for transfers between devices  299 us (38%)
  blocking collectives  170 us (21%)
  matrix products  162 us (20%)
  local copies, waits for them, and re-layouts  95.5 us (12%)
  other arithmetic  49.1 us (6%)
  between operations  14.8 us (2%)
    unnamed x17, waiting for transfers between devices  83.4 us
    reduce_scatter x1, waiting for transfers between devices, body(): lax.psum_scatter(grad_up.astype(jnp.bfloat16), 'fsdp', scatter_dimension=...  64.7 us
    reduce_scatter x1, waiting for transfers between devices, body(): lax.psum_scatter(grad_down.astype(jnp.bfloat16), 'tp', scatter_dimension=...  48.1 us
    all_gather x1, blocking collectives, fetch_attn(): lax.all_gather(w_qkv, 'fsdp', axis=0, tiled=True)  42 us
    reduce_scatter x1, waiting for transfers between devices, body(): lax.psum_scatter(grad_up.astype(jnp.bfloat16), 'tp', scatter_dimension=1,...  37.7 us
    psum x1, blocking collectives, body(): lax.psum((sum_qv, sum_up, sum_out, sum_down), 'fsdp')  37.6 us
    psum x1, blocking collectives, body(): lax.psum((gain_one_part, shift_one_part, gain_two_part, shift_two_part),...  37.5 us
    all_gather x1, blocking collectives, fetch_attn(): lax.all_gather(w_out, 'fsdp', axis=1, tiled=True)  31.8 us
  transfers between devices with their start and end apart: 14, of which 9 were waited for; matrix products, arithmetic and copies ran while one was open for 28% of the time, Pallas kernels for 0%

commit v1 on v0

v1 whole, which is shorter than its diff:
```python
import functools

import jax
import jax.numpy as jnp
from jax import lax
from jax.experimental import pallas as pl
from jax.experimental.pallas import tpu as pltpu
from jax.sharding import PartitionSpec as P

HEAD_DIM = 64
SEQ_LEN = 512
HALF = 256
EPS = 1e-05
AXES = ("fsdp", "tp")
BF = jnp.bfloat16
F32 = jnp.float32
MB = 1 << 20


def dot(left, right):
    return lax.dot_general(left, right, (((1,), (0,)), ((), ())), preferred_element_type=F32)


def dot_nt(left, right):
    return lax.dot_general(left, right, (((1,), (1,)), ((), ())), preferred_element_type=F32)


def dot_tn(left, right):
    return lax.dot_general(left, right, (((0,), (0,)), ((), ())), preferred_element_type=F32)


def whole(shape):
    zeros = (0,) * len(shape)
    return pl.BlockSpec(shape, lambda *_: zeros)


def params(limit_mb):
    return pltpu.CompilerParams(vmem_limit_bytes=limit_mb * MB)


def cost(flops, nbytes, trans=0):
    return pl.CostEstimate(flops=int(flops), bytes_accessed=int(nbytes), transcendentals=int(trans))


def unit_rows(rows):
    centre = rows - jnp.mean(rows, axis=-1, keepdims=True)
    spread = lax.rsqrt(jnp.mean(centre * centre, axis=-1, keepdims=True) + EPS)
    return centre * spread, spread


def norm_back(grad_out, unit, spread, gain):
    scaled = grad_out * gain
    inner = jnp.mean(scaled * unit, axis=-1, keepdims=True)
    return spread * (scaled - jnp.mean(scaled, axis=-1, keepdims=True) - unit * inner)


def add_sum(ref, value):
    @pl.when(pl.program_id(0) == 0)
    def _():
        ref[...] = jnp.zeros_like(ref)

    ref[...] += jnp.sum(value, axis=0, keepdims=True)


def start_kernel(x_ref, cot_ref, gain_ref, shift_ref, n1_ref, n1t_ref, cott_ref, sum_ref):
    unit, _ = unit_rows(x_ref[...].astype(F32))
    normed = unit * gain_ref[...].astype(F32) + shift_ref[...].astype(F32)
    n1_ref[...] = normed.astype(BF)
    n1t_ref[...] = normed.T.astype(BF)
    cot = cot_ref[...].astype(F32)
    cott_ref[...] = cot.T.astype(BF)
    add_sum(sum_ref, cot)


def start_call(x, cot, gain, shift):
    rows, d = x.shape
    tile = 256
    by_rows = pl.BlockSpec((tile, d), lambda i: (i, 0))
    by_cols = pl.BlockSpec((d, tile), lambda i: (0, i))
    return pl.pallas_call(
        start_kernel,
        grid=(rows // tile,),
        in_specs=[by_rows, by_rows, whole((1, d)), whole((1, d))],
        out_specs=[by_rows, by_cols, by_cols, whole((1, d))],
        out_shape=[
            jax.ShapeDtypeStruct((rows, d), BF),
            jax.ShapeDtypeStruct((d, rows), BF),
            jax.ShapeDtypeStruct((d, rows), BF),
            jax.ShapeDtypeStruct((1, d), F32),
        ],
        compiler_params=params(24),
        cost_estimate=cost(0, 10 * rows * d),
        name="start",
    )(x, cot, gain, shift)


def assemble_kernel(count, place_ref, *refs):
    pieces, out_ref, sems = refs[: 2 * count], refs[2 * count], refs[2 * count + 1]
    z, x = place_ref[0], place_ref[1]
    copies = []
    for k in range(count):
        for dx in range(2):
            slot = lax.rem(z - k + count, count) * 2 + lax.rem(x + dx, 2)
            copies.append(
                pltpu.make_async_copy(
                    pieces[dx * count + k], out_ref.at[slot], sems.at[dx * count + k]
                )
            )
    for copy in copies:
        copy.start()
    for copy in copies:
        copy.wait()


def assemble(place, near, far):
    count = len(near)
    rows, cols = near[0].shape
    out = pl.pallas_call(
        functools.partial(assemble_kernel, count),
        in_specs=[pl.BlockSpec(memory_space=pltpu.SMEM)]
        + [pl.BlockSpec(memory_space=pl.ANY)] * (2 * count),
        out_specs=pl.BlockSpec(memory_space=pl.ANY),
        out_shape=jax.ShapeDtypeStruct((2 * count, rows, cols), BF),
        scratch_shapes=[pltpu.SemaphoreType.DMA((2 * count,))],
        cost_estimate=cost(0, 8 * count * rows * cols),
        name="assemble",
    )(place, *near, *far)
    return out.reshape(2 * count * rows, cols)


HEAD_PLACES = ((0, 1, 2, 0, 0), (0, 1, 2, 64, 64), (3, 4, 3, 0, 64))


def lane_keep(tile, first):
    lanes = lax.broadcasted_iota(jnp.int32, tile.shape, 1)
    keep = (lanes >= first) & (lanes < first + HEAD_DIM)
    return jnp.where(keep, tile, jnp.zeros_like(tile))


def score_block(keys, query, start, stop, first_query):
    scores = dot_nt(keys[start:stop], query)
    if stop - 1 > first_query:
        key_idx = lax.broadcasted_iota(jnp.int32, scores.shape, 0) + start
        query_idx = lax.broadcasted_iota(jnp.int32, scores.shape, 1) + first_query
        scores = jnp.where(key_idx <= query_idx, scores, -1e30)
    return scores


def attend_kernel(n1_ref, w_ref, bias_ref, proj_ref, mixed_ref, lse_ref):
    projected = (dot(n1_ref[...], w_ref[...]) + bias_ref[...]).astype(BF)
    proj_ref[...] = projected
    outs = {}
    for head, (qt, kt, vt, qk_lane, v_lane) in enumerate(HEAD_PLACES):
        query = lane_keep(projected[:, qt * 128 : qt * 128 + 128], qk_lane) * BF(0.125)
        keys = projected[:, kt * 128 : kt * 128 + 128]
        values = projected[:, vt * 128 : vt * 128 + 128]
        for block in range(2):
            first = block * HALF
            last = first + HALF
            scores = score_block(keys, query[first:last], 0, last, first)
            top = jnp.max(scores, axis=0, keepdims=True)
            weight = jnp.exp(scores - top)
            total = jnp.sum(weight, axis=0, keepdims=True)
            mixed = dot_tn(values[0:last], weight.astype(BF)) * (1.0 / total)
            outs[head, block] = mixed[v_lane : v_lane + HEAD_DIM]
            lse_ref[0, head : head + 1, first:last] = top + jnp.log(total)
    for block in range(2):
        first = block * HALF
        rows = slice(first, first + HALF)
        single = jnp.concatenate([jnp.zeros_like(outs[2, block]), outs[2, block]], axis=0)
        pair = jnp.concatenate([outs[0, block], outs[1, block]], axis=0)
        mixed_ref[rows, 0:128] = single.T.astype(BF)
        mixed_ref[rows, 128:256] = pair.T.astype(BF)


def attend_call(n1, w, bias):
    rows, d = n1.shape
    seqs = rows // SEQ_LEN
    return pl.pallas_call(
        attend_kernel,
        grid=(seqs,),
        in_specs=[
            pl.BlockSpec((SEQ_LEN, d), lambda i: (i, 0)),
            pl.BlockSpec((d, 640), lambda i: (0, 0)),
            whole((1, 640)),
        ],
        out_specs=[
            pl.BlockSpec((SEQ_LEN, 640), lambda i: (i, 0)),
            pl.BlockSpec((SEQ_LEN, 256), lambda i: (i, 0)),
            pl.BlockSpec((1, 8, SEQ_LEN), lambda i: (i, 0, 0)),
        ],
        out_shape=[
            jax.ShapeDtypeStruct((rows, 640), BF),
            jax.ShapeDtypeStruct((rows, 256), BF),
            jax.ShapeDtypeStruct((seqs, 8, SEQ_LEN), F32),
        ],
        compiler_params=params(32),
        cost_estimate=cost(6e9, 8e6),
        name="attend",
    )(n1, w, bias)


def middle_kernel(x_ref, bias_ref, gain_ref, shift_ref, *refs):
    mixed, weights, (mid_ref, n2_ref, n2t_ref) = refs[0:4], refs[4:8], refs[8:]
    attended = bias_ref[...].astype(F32)
    for m, w in zip(mixed, weights):
        attended = attended + dot_nt(m[...], w[...])
    middle = x_ref[...].astype(F32) + attended
    mid_ref[...] = middle
    unit, _ = unit_rows(middle)
    normed = unit * gain_ref[...].astype(F32) + shift_ref[...].astype(F32)
    n2_ref[...] = normed.astype(BF)
    n2t_ref[...] = normed.T.astype(BF)


def middle_call(x, bias, gain, shift, mixed, weights):
    rows, d = x.shape
    tile = 256
    by_rows = pl.BlockSpec((tile, d), lambda i: (i, 0))
    return pl.pallas_call(
        middle_kernel,
        grid=(rows // tile,),
        in_specs=[by_rows, whole((1, d)), whole((1, d)), whole((1, d))]
        + [pl.BlockSpec((tile, 256), lambda i: (i, 0))] * 4
        + [pl.BlockSpec((d, 256), lambda i: (0, 2))] * 4,
        out_specs=[by_rows, by_rows, pl.BlockSpec((d, tile), lambda i: (0, i))],
        out_shape=[
            jax.ShapeDtypeStruct((rows, d), F32),
            jax.ShapeDtypeStruct((rows, d), BF),
            jax.ShapeDtypeStruct((d, rows), BF),
        ],
        compiler_params=params(24),
        cost_estimate=cost(2 * rows * d * 1024, 16e6),
        name="middle",
    )(x, bias, gain, shift, *mixed, *weights)


def gelu_both(value):
    size = jnp.abs(value)
    frac = 1.0 / (1.0 + (0.3275911 * 2.0**-0.5) * size)
    bell = jnp.exp(-0.5 * value * value)
    series = 0.5 * 1.061405429 * frac - 0.5 * 1.453152027
    series = series * frac + 0.5 * 1.421413741
    series = series * frac - 0.5 * 0.284496736
    series = series * frac + 0.5 * 0.254829592
    tail = series * frac * bell
    cumulative = jnp.where(value < 0, tail, 1.0 - tail)
    return value * cumulative, cumulative + value * bell * (2.0 * 3.141592653589793) ** -0.5


def store_blocks(ref, place_ref, value, count):
    z, x = place_ref[0], place_ref[1]
    size = value.shape[0] // (2 * count)
    for block in range(2 * count):
        slot = lax.rem(x + block % 2, 2) * count + lax.rem(block // 2 - z + count, count)
        ref[slot] = value[block * size : (block + 1) * size].astype(BF)


def feed_kernel(count, tokens, place_ref, n2_ref, n2t_ref, cot_ref, cott_ref, *refs):
    ups, downs, biases = refs[0:2], refs[2:4], refs[4:6]
    hidden_refs, pre_refs, gup_refs, gdown_refs, sum_refs = (
        refs[6:8],
        refs[8:10],
        refs[10:12],
        refs[12:14],
        refs[14:16],
    )
    rows = n2_ref.shape[0]
    for c in range(2):
        up, down, bias = ups[c][...], downs[c][...], biases[c][...]
        total = jnp.zeros_like(bias)
        for first in range(0, rows, tokens):
            here = slice(first, first + tokens)
            pre = dot(n2_ref[here], up) + bias
            grad_hidden = dot(cot_ref[here], down)
            hidden, slope = gelu_both(pre)
            hidden_refs[c][here] = hidden.astype(BF)
            grad_pre = (grad_hidden * slope).astype(BF)
            pre_refs[c][here] = grad_pre
            total = total + jnp.sum(grad_pre.astype(F32), axis=0, keepdims=True)
        sum_refs[c][...] = total
        store_blocks(gup_refs[c], place_ref, dot(n2t_ref[...], pre_refs[c][...]), count)
        store_blocks(gdown_refs[c], place_ref, dot(cott_ref[...], hidden_refs[c][...]), count)


def feed_call(place, count, n2, n2t, cot, cott, ups, downs, biases):
    rows, d = n2.shape
    units = ups[0].shape[1]
    tile = 256
    shard = d // (2 * count)
    cols = lambda n: pl.BlockSpec((n, tile), lambda i: (0, i))
    blocks = pl.BlockSpec((2 * count, shard, tile), lambda i: (0, 0, i))
    hid = jax.ShapeDtypeStruct((rows, units), BF)
    grad = jax.ShapeDtypeStruct((2 * count, shard, units), BF)
    total = jax.ShapeDtypeStruct((1, units), F32)
    return pl.pallas_call(
        functools.partial(feed_kernel, count, 256),
        grid=(units // tile,),
        in_specs=[
            pl.BlockSpec(memory_space=pltpu.SMEM),
            whole((rows, d)),
            whole((d, rows)),
            whole((rows, d)),
            whole((d, rows)),
        ]
        + [cols(d)] * 4
        + [cols(1)] * 2,
        out_specs=[cols(rows)] * 4 + [blocks] * 4 + [cols(1)] * 2,
        out_shape=[hid] * 4 + [grad] * 4 + [total] * 2,
        compiler_params=params(48),
        cost_estimate=cost(2 * 4 * 2 * rows * d * units, 20e6, 2 * rows * units),
        name="feed",
    )(place, n2, n2t, cot, cott, *ups, *downs, *biases)


def output_kernel(mid_ref, cot_ref, bias_ref, gain_ref, *refs):
    hidden, pre, ups, downs = refs[0:4], refs[4:8], refs[8:12], refs[12:16]
    out_ref, gmid_ref, grows_ref, growst_ref, gain_sum, shift_sum, bias_sum = refs[16:]
    mlp = bias_ref[...].astype(F32)
    grad = None
    for h, w in zip(hidden, downs):
        mlp = mlp + dot_nt(h[...], w[...])
    for g, w in zip(pre, ups):
        term = dot_nt(g[...], w[...])
        grad = term if grad is None else grad + term
    middle = mid_ref[...]
    out_ref[...] = (middle + mlp).astype(BF)
    unit, spread = unit_rows(middle)
    add_sum(gain_sum, grad * unit)
    add_sum(shift_sum, grad)
    back = norm_back(grad, unit, spread, gain_ref[...].astype(F32))
    grad_middle = cot_ref[...].astype(F32) + back
    gmid_ref[...] = grad_middle
    rows = grad_middle.astype(BF)
    grows_ref[...] = rows
    growst_ref[...] = grad_middle.T.astype(BF)
    add_sum(bias_sum, rows.astype(F32))


def output_call(middle, cot, bias, gain, hidden, pre, ups, downs):
    rows, d = middle.shape
    units = ups[0].shape[1]
    tile = 256
    by_rows = pl.BlockSpec((tile, d), lambda i: (i, 0))
    kept = pl.BlockSpec((d, units), lambda i: (0, 0), pipeline_mode=pl.Buffered(1))
    total = jax.ShapeDtypeStruct((1, d), F32)
    return pl.pallas_call(
        output_kernel,
        grid=(rows // tile,),
        in_specs=[by_rows, by_rows, whole((1, d)), whole((1, d))]
        + [pl.BlockSpec((tile, units), lambda i: (i, 0))] * 8
        + [kept] * 8,
        out_specs=[by_rows] * 3 + [pl.BlockSpec((d, tile), lambda i: (0, i))] + [whole((1, d))] * 3,
        out_shape=[
            jax.ShapeDtypeStruct((rows, d), BF),
            jax.ShapeDtypeStruct((rows, d), F32),
            jax.ShapeDtypeStruct((rows, d), BF),
            jax.ShapeDtypeStruct((d, rows), BF),
            total,
            total,
            total,
        ],
        compiler_params=params(48),
        cost_estimate=cost(2 * 8 * rows * d * units, 34e6),
        name="output",
    )(middle, cot, bias, gain, *hidden, *pre, *ups, *downs)


def attend_back_kernel(
    count,
    place_ref,
    grows_ref,
    growst_ref,
    n1t_ref,
    w_ref,
    proj_ref,
    mixed_ref,
    lse_ref,
    gproj_ref,
    gw_ref,
    sum_ref,
    total,
):
    step = pl.program_id(0)
    projected = proj_ref[...]
    grad_mixed = dot(grows_ref[...], w_ref[...]).astype(BF)
    parts = {}
    for head, (qt, kt, vt, qk_lane, v_lane) in enumerate(HEAD_PLACES):
        mt = 0 if head == 2 else 1
        query = lane_keep(projected[:, qt * 128 : qt * 128 + 128], qk_lane) * BF(0.125)
        keys = projected[:, kt * 128 : kt * 128 + 128]
        values = projected[:, vt * 128 : vt * 128 + 128]
        grads = lane_keep(grad_mixed[:, mt * 128 : mt * 128 + 128], v_lane)
        gkeys, gvalues = [None, None], [None, None]
        for block in range(2):
            first = block * HALF
            last = first + HALF
            qb, gb = query[first:last], grads[first:last]
            scores = score_block(keys, qb, 0, last, first)
            probs = jnp.exp(scores - lse_ref[0, head : head + 1, first:last])
            gprobs = dot_nt(values[0:last], gb)
            both = probs * gprobs
            delta = jnp.sum(both, axis=0, keepdims=True)
            gscores = (both - probs * delta).astype(BF)
            gq = dot_tn(keys[0:last], gscores) * 0.125
            parts["q", head, block] = gq[qk_lane : qk_lane + HEAD_DIM]
            gk = dot(gscores, qb)
            gv = dot(probs.astype(BF), gb)
            for b in range(block + 1):
                part = slice(b * HALF, b * HALF + HALF)
                gkeys[b] = gk[part] if gkeys[b] is None else gkeys[b] + gk[part]
                gvalues[b] = gv[part] if gvalues[b] is None else gvalues[b] + gv[part]
        parts["k", head] = gkeys
        parts["v", head] = gvalues
    for block in range(2):
        rows = slice(block * HALF, block * HALF + HALF)
        pair = jnp.concatenate([parts["q", 0, block], parts["q", 1, block]], axis=0).T
        lone = parts["q", 2, block]
        lone = jnp.concatenate([lone, jnp.zeros_like(lone)], axis=0).T
        gproj_ref[rows, 0:128] = pair.astype(BF)
        gproj_ref[rows, 128:256] = (parts["k", 0][block] + parts["k", 1][block]).astype(BF)
        gproj_ref[rows, 256:384] = (parts["v", 0][block] + parts["v", 1][block]).astype(BF)
        gproj_ref[rows, 384:512] = (lone + parts["v", 2][block]).astype(BF)
        gproj_ref[rows, 512:640] = parts["k", 2][block].astype(BF)
    gproj = gproj_ref[...]
    add_sum(sum_ref, gproj.astype(F32))
    grad_a = dot(n1t_ref[...], gproj)
    grad_b = dot(growst_ref[...], mixed_ref[...])
    grad = jnp.concatenate(
        [grad_a[:, 0:512], grad_a[:, 512:640] + grad_b[:, 0:128], grad_b[:, 128:256]], axis=1
    )

    @pl.when(step == 0)
    def _():
        total[...] = grad

    @pl.when(step > 0)
    def _():
        total[...] += grad

    @pl.when(step == pl.num_programs(0) - 1)
    def _():
        store_blocks(gw_ref, place_ref, total[...], count)


def attend_back_call(place, count, grows, growst, n1t, w, proj, mixed, lse):
    rows, d = grows.shape
    seqs = rows // SEQ_LEN
    shard = d // (2 * count)
    by_rows = lambda n: pl.BlockSpec((SEQ_LEN, n), lambda i: (i, 0))
    by_cols = pl.BlockSpec((d, SEQ_LEN), lambda i: (0, i))
    return pl.pallas_call(
        functools.partial(attend_back_kernel, count),
        grid=(seqs,),
        in_specs=[
            pl.BlockSpec(memory_space=pltpu.SMEM),
            by_rows(d),
            by_cols,
            by_cols,
            pl.BlockSpec((d, 256), lambda i: (0, 2)),
            by_rows(640),
            by_rows(256),
            pl.BlockSpec((1, 8, SEQ_LEN), lambda i: (i, 0, 0)),
        ],
        out_specs=[by_rows(640), whole((2 * count, shard, 768)), whole((1, 640))],
        out_shape=[
            jax.ShapeDtypeStruct((rows, 640), BF),
            jax.ShapeDtypeStruct((2 * count, shard, 768), BF),
            jax.ShapeDtypeStruct((1, 640), F32),
        ],
        scratch_shapes=[pltpu.VMEM((d, 768), F32)],
        compiler_params=params(40),
        cost_estimate=cost(10e9, 12e6),
        name="attend_back",
    )(place, grows, growst, n1t, w, proj, mixed, lse)


def finish_kernel(x_ref, gmid_ref, gain_ref, *refs):
    gproj, weights, (out_ref, gain_sum, shift_sum) = refs[0:4], refs[4:8], refs[8:]
    grad = None
    for g, w in zip(gproj, weights):
        term = dot_nt(g[...], w[...])
        grad = term if grad is None else grad + term
    unit, spread = unit_rows(x_ref[...].astype(F32))
    add_sum(gain_sum, grad * unit)
    add_sum(shift_sum, grad)
    back = norm_back(grad, unit, spread, gain_ref[...].astype(F32))
    out_ref[...] = (gmid_ref[...] + back).astype(BF)


def finish_call(x, gmid, gain, gproj, weights):
    rows, d = x.shape
    tile = 256
    by_rows = pl.BlockSpec((tile, d), lambda i: (i, 0))
    total = jax.ShapeDtypeStruct((1, d), F32)
    return pl.pallas_call(
        finish_kernel,
        grid=(rows // tile,),
        in_specs=[by_rows, by_rows, whole((1, d))]
        + [pl.BlockSpec((tile, 640), lambda i: (i, 0))] * 4
        + [pl.BlockSpec((d, 640), lambda i: (0, 0))] * 4,
        out_specs=[by_rows, whole((1, d)), whole((1, d))],
        out_shape=[jax.ShapeDtypeStruct((rows, d), BF), total, total],
        compiler_params=params(32),
        cost_estimate=cost(2 * 4 * rows * d * 640, 16e6),
        name="finish",
    )(x, gmid, gain, *gproj, *weights)


class Links:
    def __init__(self, mesh):
        self.count = mesh.shape["fsdp"] // 2
        places = [
            (z, x, y, c)
            for z in range(self.count)
            for x in range(2)
            for y in range(2)
            for c in range(2)
        ]

        def index(z, x, y, c):
            return ((z * 2 + x) * 2 + y) * 2 + c

        def pairs(move):
            return [(index(*p), index(*move(*p))) for p in places]

        self.core = pairs(lambda z, x, y, c: (z, x, y, 1 - c))
        self.y = pairs(lambda z, x, y, c: (z, x, 1 - y, c))
        self.x = pairs(lambda z, x, y, c: (z, 1 - x, y, c))
        self.ring = pairs(lambda z, x, y, c: ((z + 1) % self.count, x, y, c))
        self.bits = []
        bit = 1
        while bit < self.count:
            self.bits.append(pairs(lambda z, x, y, c, b=bit: (z ^ b, x, y, c)))
            bit *= 2

    @staticmethod
    def send(value, pairs):
        return lax.ppermute(value, AXES, pairs)


def gather(links, place, shard):
    near = [shard]
    for _ in range(links.count - 1):
        near.append(links.send(near[-1], links.ring))
    far = [links.send(v, links.x) for v in near]
    own = assemble(place, near, far)
    over = links.send(own, links.y)
    return [own, links.send(own, links.core), over, links.send(over, links.core)]


def plus(a, b, kind=BF):
    return (a.astype(F32) + b.astype(F32)).astype(kind)


def scatter_pair(links, own, other):
    return plus(own, links.send(other, links.core))


def scatter_rest(links, here, there):
    n = links.count
    both = links.send(there, links.y)
    away = plus(here[n:], both[n:])
    home = plus(here[:n], both[:n])
    home = plus(home, links.send(away, links.x))
    held = home[n - 1]
    for k in range(n - 2, -1, -1):
        held = plus(home[k], links.send(held, links.ring), F32 if k == 0 else BF)
    return held


def sum_all(links, rep, groups):
    n = rep.shape[0]
    got = links.send(jnp.concatenate([rep, groups[1], groups[3]]), links.core)
    width = groups.shape[1]
    rep = rep + got[:n]
    here = groups[0] + got[n : n + width]
    there = groups[2] + got[n + width :]
    got = links.send(jnp.concatenate([rep, there]), links.y)
    vec = jnp.concatenate([rep, here]) + got
    vec = vec + links.send(vec, links.x)
    for pairs in links.bits:
        vec = vec + links.send(vec, pairs)
    return vec[:n], vec[n:]


def pack_attn(w_qkv, w_out):
    q, k, v, o = w_qkv[:, 0], w_qkv[:, 1], w_qkv[:, 2], w_out.T
    return jnp.concatenate(
        [q[:, :128], k[:, :128], v[:, :128], q[:, 128:], v[:, 128:], k[:, 128:], o[:, 128:], o[:, :128]],
        axis=1,
    )


def unpack_attn(g):
    q = jnp.concatenate([g[:, 0:128], g[:, 384:448]], axis=1)
    k = jnp.concatenate([g[:, 128:256], g[:, 512:576]], axis=1)
    v = jnp.concatenate([g[:, 256:384], g[:, 448:512]], axis=1)
    o = jnp.concatenate([g[:, 640:768], g[:, 576:640]], axis=1)
    return jnp.stack([q, k, v], axis=1), o.T


def body(
    links,
    layer_input,
    w_qkv,
    bias_qv,
    w_out,
    bias_out,
    gain_attn,
    shift_attn,
    gain_mlp,
    shift_mlp,
    w_up,
    bias_up,
    w_down,
    bias_down,
    cotangent,
):
    fsdp = lax.axis_index("fsdp")
    place = jnp.stack([fsdp // 2, fsdp % 2]).astype(jnp.int32)
    row = lambda v: v.reshape(1, -1)
    count = links.count

    small = jnp.concatenate([bias_qv[0], bias_qv[1], bias_up])
    small_y = links.send(small, links.y)
    smalls = [small, links.send(small, links.core), small_y, links.send(small_y, links.core)]
    heads = bias_qv.shape[1]

    attn_w = gather(links, place, pack_attn(w_qkv, w_out))
    up_w = gather(links, place, w_up)
    down_w = gather(links, place, w_down.T)

    n1, n1t, cott, sum_down = start_call(layer_input, cotangent, row(gain_attn), row(shift_attn))

    proj, mixed, lse = [], [], []
    for j in range(4):
        bq, bv = smalls[j][:heads].astype(F32), smalls[j][heads : 2 * heads].astype(F32)
        none = jnp.zeros((128,), F32)
        bias = jnp.concatenate([bq[:128], none, bv[:128], bq[128:], bv[128:], none])
        p, m, s = attend_call(n1, attn_w[j], row(bias))
        proj.append(p)
        mixed.append(m)
        lse.append(s)

    middle, n2, n2t = middle_call(
        layer_input, row(bias_out), row(gain_mlp), row(shift_mlp), mixed, attn_w
    )

    hidden, pre, sum_up = [None] * 4, [None] * 4, [None] * 4
    half_up, half_down = [None] * 2, [None] * 2
    for dy in (1, 0):
        js = (2 * dy, 2 * dy + 1)
        out = feed_call(
            place,
            count,
            n2,
            n2t,
            cotangent,
            cott,
            [up_w[j] for j in js],
            [down_w[j] for j in js],
            [row(smalls[j][2 * heads :].astype(F32)) for j in js],
        )
        for c, j in enumerate(js):
            hidden[j], pre[j], sum_up[j] = out[c], out[2 + c], out[8 + c]
        half_up[dy] = scatter_pair(links, out[4], out[5])
        half_down[dy] = scatter_pair(links, out[6], out[7])

    layer_output, gmid, grows, growst, gain_two, shift_two, sum_out = output_call(
        middle, cotangent, row(bias_down), row(gain_mlp), hidden, pre, up_w, down_w
    )
    grad_up = scatter_rest(links, half_up[0], half_up[1])
    grad_down = scatter_rest(links, half_down[0], half_down[1])

    gproj, gattn, sum_proj = [None] * 4, [None] * 4, [None] * 4
    for j in (3, 2, 1, 0):
        gproj[j], gattn[j], sum_proj[j] = attend_back_call(
            place, count, grows, growst, n1t, attn_w[j], proj[j], mixed[j], lse[j]
        )
    half_attn = [scatter_pair(links, gattn[2 * dy], gattn[2 * dy + 1]) for dy in range(2)]
    grad_attn = scatter_rest(links, half_attn[0], half_attn[1])

    grad_input, gain_one, shift_one = finish_call(
        layer_input, gmid, row(gain_attn), gproj, attn_w
    )

    d = layer_input.shape[1]
    groups = []
    for j in range(4):
        s = sum_proj[j][0]
        groups.append(
            jnp.concatenate([s[0:128], s[384:448], s[256:384], s[448:512], sum_up[j][0]])
        )
    rep = jnp.concatenate(
        [v[0] for v in (sum_out, sum_down, gain_one, shift_one, gain_two, shift_two)]
    )
    rep, own = sum_all(links, rep, jnp.stack(groups))
    total_out, total_down, gain_one, shift_one, gain_two, shift_two = rep.reshape(6, d)
    total_qv, total_up = own[: 2 * heads].reshape(2, heads), own[2 * heads :]

    shard_qkv, shard_out = unpack_attn(grad_attn)
    return (
        layer_output,
        grad_input,
        shard_qkv,
        total_qv,
        shard_out,
        total_out,
        gain_one,
        shift_one,
        gain_two,
        shift_two,
        grad_up,
        total_up,
        grad_down.T,
        total_down,
    )


def solution(mesh):
    tokens = P(("fsdp", "tp"), None)
    placed = (
        tokens,
        P("fsdp", None, "tp"),
        P(None, "tp"),
        P("tp", "fsdp"),
        P(),
        P(),
        P(),
        P(),
        P(),
        P("fsdp", "tp"),
        P("tp"),
        P("tp", "fsdp"),
        P(),
        tokens,
    )
    return jax.shard_map(
        functools.partial(body, Links(mesh)),
        mesh=mesh,
        in_specs=placed,
        out_specs=(
            tokens,
            tokens,
            P("fsdp", None, "tp"),
            P(None, "tp"),
            P("tp", "fsdp"),
            P(),
            P(),
            P(),
            P(),
            P(),
            P("fsdp", "tp"),
            P("tp"),
            P("tp", "fsdp"),
            P(),
        ),
        check_vma=False,
    )
```

time: 796 us -> 532 us (0.67)
  Pallas kernels: 0 us -> 247 us
  blocking collectives: 170 us -> 0 us
  matrix products: 162 us -> 0 us
  waiting for transfers between devices: 299 us -> 138 us
  starting transfers between devices: 1.09 us -> 51.4 us
  other arithmetic: 49.1 us -> 17.7 us
  local copies, waits for them, and re-layouts: 95.5 us -> 71.4 us
  between operations: 14.8 us -> 2.1 us
    pallas_call x0 -> x17, Pallas kernels: none -> 247 us  [the longest x3 113 us: assemble(): pl.pallas_call(functools.partial(assemble_kernel, count), in_specs=[pl.Bl...]
    reduce_scatter x5 -> x0, waiting for transfers between devices: 169 us -> none  [the longest x1 64.7 us: body(): lax.psum_scatter(grad_up.astype(jnp.bfloat16), 'fsdp', scatter_dimension=...]
    dot_general x18 -> x0, matrix products: 162 us -> none  [the longest x3 25.3 us: against(): lax.dot_general(left, right, (((1,), (1,)), ((), ())), preferred_element_...]
    ppermute x0 -> x59, waiting for transfers between devices: none -> 138 us  [send(): return lax.ppermute(value, AXES, pairs)]
    psum x3 -> x0, blocking collectives: 85.8 us -> none  [the longest x1 37.6 us: body(): lax.psum((sum_qv, sum_up, sum_out, sum_down), 'fsdp')]
    all_gather x4 -> x0, blocking collectives: 84 us -> none  [the longest x1 42 us: fetch_attn(): lax.all_gather(w_qkv, 'fsdp', axis=0, tiled=True)]
    unnamed x17 -> x0, waiting for transfers between devices: 83.4 us -> none
    ppermute x0 -> x59, starting transfers between devices: none -> 51.4 us  [send(): return lax.ppermute(value, AXES, pairs)]
  transfers between devices with their start and end apart: 14 -> 59, of which waited for: 9 -> 20; matrix products, arithmetic and copies ran while one was open for 28% -> 8% of each run, Pallas kernels for 0% -> 32%
where the time goes in v1:
time: 532 us; the launch traced here: 528 us
  Pallas kernels  247 us (46%)
  waiting for transfers between devices  138 us (26%)
  local copies, waits for them, and re-layouts  71.4 us (13%)
  starting transfers between devices  51.4 us (10%)
  other arithmetic  17.7 us (3%)
    ppermute x59, waiting for transfers between devices, send(): return lax.ppermute(value, AXES, pairs)  138 us
    pallas_call x3, Pallas kernels, assemble(): pl.pallas_call(functools.partial(assemble_kernel, count), in_specs=[pl.Bl...  113 us
    ppermute x59, starting transfers between devices, send(): return lax.ppermute(value, AXES, pairs)  51.4 us
    unnamed x203, local copies, waits for them, and re-layouts  49.9 us
    pallas_call x4, Pallas kernels, attend_back_call(): pl.pallas_call(functools.partial(attend_back_kernel, count), grid=(seqs,)...  41.9 us
    pallas_call x2, Pallas kernels, feed_call(): pl.pallas_call(functools.partial(feed_kernel, count, 256), grid=(units //...  39.6 us
    pallas_call x1, Pallas kernels, output_call(): pl.pallas_call(output_kernel, grid=(rows // tile,), in_specs=[by_rows, by...  19.1 us
    pallas_call x4, Pallas kernels, attend_call(): pl.pallas_call(attend_kernel, grid=(seqs,), in_specs=[pl.BlockSpec((SEQ_L...  17.9 us
  transfers between devices with their start and end apart: 59, of which 20 were waited for; matrix products, arithmetic and copies ran while one was open for 8% of the time, Pallas kernels for 32%

profile of v1, /device:TPU:0, one launch (start us, length us, event | category | flops | bytes accessed | tf_op | source)
XLA Modules:
  0.0 527.6 jit_solution(14254994969665320918)
XLA Ops:
  2.7 3.1 collective-permute-start
  5.8 5.9 %collective-permute-done.refs_1_ = bf16[96,768]{1,0:T(8,128)(2,1)S(1)} collective-permute-done((bf16[96,768]{1,0:T(8,128)(2,1)S(1)}, bf16[96,768]{1,0:T(8,128)(2,1)S(1)}, u32[]{:S(2)}, u32[]{:S(2)}) %collective-permute-start) | collective-permute-done | bytes 147488 | tf_op jit(solution)/shard_map/ppermute | solution.py:539
  11.7 6.9 %collective-permute-done.1.refs_2_ = bf16[96,768]{1,0:T(8,128)(2,1)S(1)} collective-permute-done((bf16[96,768]{1,0:T(8,128)(2,1)S(1)}, bf16[96,768]{1,0:T(8,128)(2,1)S(1)}, u32[]{:S(2)}, u32[]{:S(2)}) %collective-permute-start.1) | collective-permute-done | bytes 147488 | tf_op jit(solution)/shard_map/ppermute | solution.py:539
  22.1 3.4 collective-permute-done.2.refs_3_
  43.7 37.6 %assemble.3 = bf16[8,96,768]{2,1,0:T(8,128)(2,1)} custom-call(s32[2]{0:T(128)} %pad_add_fusion.place_ref, bf16[96,768]{1,0:T(8,128)(2,1)} %copy-done.71, bf16[96,768]{1,0:T(8,128)(2,1)} %copy-done.75, bf16[96,768]{1,0:T(8,128)(2,1)} %copy-done.77, bf16[96,768]{1,0:T(8,128)(2,1)} %copy-done.78, bf16[96,768]{1,0:T(8,128)(2,1)} %copy-done.79, ...), custom_call_target="tpu_custom_call" | custom-call | bytes 2359296 | tf_op jit(solution)/shard_map/assemble/pallas_call | solution.py:118
  82.9 3.5 collective-permute-start.14
  86.4 4.1 collective-permute-done.22.refs_2_
  107.4 37.7 %assemble.5 = bf16[8,96,768]{2,1,0:T(8,128)(2,1)} custom-call(s32[2]{0:T(128)} %pad_add_fusion.place_ref, bf16[96,768]{1,0:T(8,128)(2,1)} %bitcast.122, bf16[96,768]{1,0:T(8,128)(2,1)} %copy-done.74, bf16[96,768]{1,0:T(8,128)(2,1)} %copy-done.83, bf16[96,768]{1,0:T(8,128)(2,1)} %copy-done.84, bf16[96,768]{1,0:T(8,128)(2,1)} %copy-done.76, ...), custom_call_target="tpu_custom_call" | custom-call | bytes 2359296 | tf_op jit(solution)/shard_map/assemble/pallas_call | solution.py:118
  146.8 37.6 %assemble.4 = bf16[8,96,768]{2,1,0:T(8,128)(2,1)} custom-call(s32[2]{0:T(128)} %pad_add_fusion.place_ref, bf16[96,768]{1,0:T(8,128)(2,1)} %refs_0_.1, bf16[96,768]{1,0:T(8,128)(2,1)} %collective-permute-done.13.refs_1_, bf16[96,768]{1,0:T(8,128)(2,1)} %collective-permute-done.14.refs_2_, bf16[96,768]{1,0:T(8,128)(2,1)} %collective-permute-done.15.refs_3_, ...), custom_call_target="tpu_custom_call" | custom-call | bytes 2359296 | tf_op jit(solution)/shard_map/assemble/pallas_call | solution.py:118
  193.2 4.5 attend.4
  199.4 4.5 attend.6
  205.1 7.7 %collective-permute-done.29.refs_0_.refs_10_ = bf16[768,768]{1,0:T(8,128)(2,1)} collective-permute-done((bf16[768,768]{1,0:T(8,128)(2,1)}, bf16[768,768]{1,0:T(8,128)(2,1)}, u32[]{:S(2)}, u32[]{:S(2)}) %collective-permute-start.29) | collective-permute-done | bytes 1179680 | tf_op jit(solution)/shard_map/ppermute | solution.py:539
  212.8 4.5 attend.5
  217.9 4.5 attend.7
  224.1 4.0 middle.1
  233.6 20.3 %feed.3 = (bf16[1024,768]{1,0:T(8,128)(2,1)}, bf16[1024,768]{1,0:T(8,128)(2,1)}, bf16[1024,768]{1,0:T(8,128)(2,1)}, bf16[1024,768]{1,0:T(8,128)(2,1)}, bf16[8,96...) custom-call(s32[2]{0:T(128)S(1)} %copy-done.17, ...), custom_call_target="tpu_custom_call" | custom-call | flops 9663676416 | bytes 20000000 | tf_op jit(solution)/shard_map/feed/pallas_call | solution.py:296
  256.7 19.3 %feed.2 = (bf16[1024,768]{1,0:T(8,128)(2,1)}, bf16[1024,768]{1,0:T(8,128)(2,1)}, bf16[1024,768]{1,0:T(8,128)(2,1)}, bf16[1024,768]{1,0:T(8,128)(2,1)}, bf16[8,96...) custom-call(s32[2]{0:T(128)S(1)} %copy-done.17, ...), custom_call_target="tpu_custom_call" | custom-call | flops 9663676416 | bytes 20000000 | tf_op jit(solution)/shard_map/feed/pallas_call | solution.py:296
  280.2 19.1 %output.1 = (bf16[1024,768]{1,0:T(8,128)(2,1)}, f32[1024,768]{1,0:T(8,128)}, bf16[1024,768]{1,0:T(8,128)(2,1)}, bf16[768,1024]{1,0:T(8,128)(2,1)}, f32[1,768]{1,...) custom-call(f32[1024,768]{1,0:T(8,128)} %copy-done.33, bf16[1024,768]{1,0:T(8,128)(2,1)} %cot_ref.7, ...), custom_call_target="tpu_custom_call" | custom-call | flops 9663676416 | bytes 34000000 | tf_op jit(solution)/shard_map/output/pallas_call | solution.py:347
  306.8 10.3 %attend_back.6 = (bf16[1024,640]{1,0:T(8,128)(2,1)S(1)}, bf16[8,96,768]{2,1,0:T(8,128)(2,1)S(1)}, f32[1,640]{1,0:T(1,128)S(1)}) custom-call(s32[2]{0:T(128)S(1)} %copy-done.17, bf16[1024,768]{1,0:T(8,128)(2,1)S(1)} %copy-done.51, bf16[768,1024]{1,0:T(8,128)(2,1)S(1)} %copy-done.53, bf16[768,1024]{1,0:T(8,128)(2,1)S(1)} %copy-done.35, ...), custom_call_target="tpu_custom_call" | custom-call | flops 10000000000 | bytes 12000000 | tf_op jit(solution)/shard_map/attend_back/pallas_call | solution.py:452
  320.8 10.1 %attend_back.4 = (bf16[1024,640]{1,0:T(8,128)(2,1)S(1)}, bf16[8,96,768]{2,1,0:T(8,128)(2,1)S(1)}, f32[1,640]{1,0:T(1,128)S(1)}) custom-call(s32[2]{0:T(128)S(1)} %copy-done.17, bf16[1024,768]{1,0:T(8,128)(2,1)S(1)} %copy-done.52, bf16[768,1024]{1,0:T(8,128)(2,1)S(1)} %copy-done.53, bf16[768,1024]{1,0:T(8,128)(2,1)S(1)} %copy-done.36, ...), custom_call_target="tpu_custom_call" | custom-call | flops 10000000000 | bytes 12000000 | tf_op jit(solution)/shard_map/attend_back/pallas_call | solution.py:452
  333.2 11.4 %attend_back.7 = (bf16[1024,640]{1,0:T(8,128)(2,1)S(1)}, bf16[8,96,768]{2,1,0:T(8,128)(2,1)}, f32[1,640]{1,0:T(1,128)S(1)}) custom-call(s32[2]{0:T(128)S(1)} %copy-done.17, bf16[1024,768]{1,0:T(8,128)(2,1)S(1)} %copy-done.52, bf16[768,1024]{1,0:T(8,128)(2,1)S(1)} %copy-done.53, bf16[768,1024]{1,0:T(8,128)(2,1)S(1)} %copy-done.36, ...), custom_call_target="tpu_custom_call" | custom-call | flops 10000000000 | bytes 12000000 | tf_op jit(solution)/shard_map/attend_back/pallas_call | solution.py:452
  345.8 10.1 %attend_back.5 = (bf16[1024,640]{1,0:T(8,128)(2,1)S(1)}, bf16[8,96,768]{2,1,0:T(8,128)(2,1)S(1)}, f32[1,640]{1,0:T(1,128)S(1)}) custom-call(s32[2]{0:T(128)S(1)} %copy-done.17, bf16[1024,768]{1,0:T(8,128)(2,1)S(1)} %copy-done.52, bf16[768,1024]{1,0:T(8,128)(2,1)S(1)} %copy-done.54, bf16[768,1024]{1,0:T(8,128)(2,1)S(1)} %copy-done.36, ...), custom_call_target="tpu_custom_call" | custom-call | flops 10000000000 | bytes 12000000 | tf_op jit(solution)/shard_map/attend_back/pallas_call | solution.py:452
  360.9 8.5 %finish.1 = (bf16[1024,768]{1,0:T(8,128)(2,1)}, f32[1,768]{1,0:T(1,128)S(1)}, f32[1,768]{1,0:T(1,128)S(1)}) custom-call(bf16[1024,768]{1,0:T(8,128)(2,1)S(1)} %copy-done.1, f32[1024,768]{1,0:T(8,128)S(1)} %copy-done.48, bf16[1,768]{1,0:T(2,128)(2,1)S(1)} %reshape.148.gain_ref, bf16[1024,640]{1,0:T(8,128)(2,1)S(1)} %get-tuple-element.99.refs_0_, ...), custom_call_target="tpu_custom_call" | custom-call | flops 4026531840 | bytes 16000000 | tf_op jit(solution)/shard_map/finish/pallas_call | solution.py:496
  386.4 3.3 collective-permute-done.41
  390.3 3.3 collective-permute-done.42
  414.3 21.2 %collective-permute-done.54 = bf16[8,96,768]{2,1,0:T(8,128)(2,1)S(1)} collective-permute-done((bf16[8,96,768]{2,1,0:T(8,128)(2,1)S(1)}, bf16[8,96,768]{2,1,0:T(8,128)(2,1)S(1)}, u32[]{:S(2)}, u32[]{:S(2)}) %collective-permute-start.54) | collective-permute-done | bytes 1179680 | tf_op jit(solution)/shard_map/ppermute | solution.py:539
  436.5 24.2 %collective-permute-done.47 = bf16[8,96,768]{2,1,0:T(8,128)(2,1)S(1)} collective-permute-done((bf16[8,96,768]{2,1,0:T(8,128)(2,1)S(1)}, bf16[8,96,768]{2,1,0:T(8,128)(2,1)S(1)}, u32[]{:S(2)}, u32[]{:S(2)}) %collective-permute-start.47) | collective-permute-done | bytes 1179680 | tf_op jit(solution)/shard_map/ppermute | solution.py:539
  461.5 23.6 %collective-permute-done.35 = bf16[8,96,768]{2,1,0:T(8,128)(2,1)S(1)} collective-permute-done((bf16[8,96,768]{2,1,0:T(8,128)(2,1)S(1)}, bf16[8,96,768]{2,1,0:T(8,128)(2,1)S(1)}, u32[]{:S(2)}, u32[]{:S(2)}) %collective-permute-start.35) | collective-permute-done | bytes 1179680 | tf_op jit(solution)/shard_map/ppermute | solution.py:539
  489.2 10.4 %collective-permute-done.36 = bf16[4,96,768]{2,1,0:T(8,128)(2,1)S(1)} collective-permute-done((bf16[4,96,768]{2,1,0:T(8,128)(2,1)S(1)}, bf16[4,96,768]{2,1,0:T(8,128)(2,1)S(1)}, u32[]{:S(2)}, u32[]{:S(2)}) %collective-permute-start.36) | collective-permute-done | bytes 589856 | tf_op jit(solution)/shard_map/ppermute | solution.py:539
  505.0 3.4 collective-permute-done.37
  512.0 5.1 collective-permute-done.38
  519.2 4.9 collective-permute-done.39
  (423 shorter events, 147.3 us)
Async XLA Ops:
  18.6 23.7 %collective-permute-start.3 = (bf16[96,768]{1,0:T(8,128)(2,1)S(1)}, bf16[96,768]{1,0:T(8,128)(2,1)S(1)}, u32[]{:S(2)}, u32[]{:S(2)}) collective-permute-start(bf16[96,768]{1,0:T(8,128)(2,1)S(1)} %concatenate.49.refs_0_), channel_id=1, source_target_pairs={{0,4},{1,5},{2,6},{3,7},{4,0},{5,1},{6,2},{7,3},{8,12},{9,13},{10,... | collective-permute-start | bytes 442376 | tf_op jit(solution)/shard_map/ppermute | solution.py:539
  20.1 22.2 %collective-permute-start.4 = (bf16[96,768]{1,0:T(8,128)(2,1)S(1)}, bf16[96,768]{1,0:T(8,128)(2,1)S(1)}, u32[]{:S(2)}, u32[]{:S(2)}) collective-permute-start(bf16[96,768]{1,0:T(8,128)(2,1)S(1)} %collective-permute-done.refs_1_), channel_id=1, source_target_pairs={{0,4},{1,5},{2,6},{3,7},{4,0},{5,1},{6,2},{7,3},{8,12},{9,13},{10,... | collective-permute-start | bytes 442376 | tf_op jit(solution)/shard_map/ppermute | solution.py:539
  20.7 21.8 %collective-permute-start.5 = (bf16[96,768]{1,0:T(8,128)(2,1)S(1)}, bf16[96,768]{1,0:T(8,128)(2,1)S(1)}, u32[]{:S(2)}, u32[]{:S(2)}) collective-permute-start(bf16[96,768]{1,0:T(8,128)(2,1)S(1)} %collective-permute-done.1.refs_2_), channel_id=1, source_target_pairs={{0,4},{1,5},{2,6},{3,7},{4,0},{5,1},{6,2},{7,3},{8,12},{9,13},{10,... | collective-permute-start | bytes 442376 | tf_op jit(solution)/shard_map/ppermute | solution.py:539
  25.6 17.5 %collective-permute-start.6 = (bf16[96,768]{1,0:T(8,128)(2,1)S(1)}, bf16[96,768]{1,0:T(8,128)(2,1)S(1)}, u32[]{:S(2)}, u32[]{:S(2)}) collective-permute-start(bf16[96,768]{1,0:T(8,128)(2,1)S(1)} %collective-permute-done.2.refs_3_), channel_id=1, source_target_pairs={{0,4},{1,5},{2,6},{3,7},{4,0},{5,1},{6,2},{7,3},{8,12},{9,13},{10,... | collective-permute-start | bytes 442376 | tf_op jit(solution)/shard_map/ppermute | solution.py:539
  28.6 52.7 %collective-permute-start.10 = (bf16[1152]{0:T(1024)(128)(2,1)S(1)}, bf16[1152]{0:T(1024)(128)(2,1)S(1)}, u32[]{:S(2)}, u32[]{:S(2)}) collective-permute-start(bf16[1152]{0:T(1024)(128)(2,1)S(1)} %concatenate.51), channel_id=1, source_target_pairs={{0,2},{1,3},{2,0},{3,1},{4,6},{5,7},{6,4},{7,5},{8,10},{9,11},{10,... | collective-permute-start | bytes 6920 | tf_op jit(solution)/shard_map/ppermute | solution.py:539
  42.3 40.5 %collective-permute-start.8 = (bf16[1152]{0:T(1024)(128)(2,1)S(1)}, bf16[1152]{0:T(1024)(128)(2,1)S(1)}, u32[]{:S(2)}, u32[]{:S(2)}) collective-permute-start(bf16[1152]{0:T(1024)(128)(2,1)S(1)} %concatenate.51), channel_id=1, source_target_pairs={{0,1},{1,0},{2,3},{3,2},{4,5},{5,4},{6,7},{7,6},{8,9},{9,8},{10,11... | collective-permute-start | bytes 6920 | tf_op jit(solution)/shard_map/ppermute | solution.py:539
  42.4 39.5 %collective-permute-start.21 = (bf16[96,768]{1,0:T(8,128)(2,1)S(1)}, bf16[96,768]{1,0:T(8,128)(2,1)S(1)}, u32[]{:S(2)}, u32[]{:S(2)}) collective-permute-start(bf16[96,768]{1,0:T(8,128)(2,1)S(1)} %bitcast.123), channel_id=1, source_target_pairs={{0,8},{1,9},{2,10},{3,11},{4,12},{5,13},{6,14},{7,15},{8,16},{9,17... | collective-permute-start | bytes 442376 | tf_op jit(solution)/shard_map/ppermute | solution.py:539
  42.5 51.6 %collective-permute-start.24 = (bf16[96,768]{1,0:T(8,128)(2,1)S(1)}, bf16[96,768]{1,0:T(8,128)(2,1)S(1)}, u32[]{:S(2)}, u32[]{:S(2)}) collective-permute-start(bf16[96,768]{1,0:T(8,128)(2,1)S(1)} %bitcast.124), channel_id=1, source_target_pairs={{0,4},{1,5},{2,6},{3,7},{4,0},{5,1},{6,2},{7,3},{8,12},{9,13},{10,... | collective-permute-start | bytes 442376 | tf_op jit(solution)/shard_map/ppermute | solution.py:539
  43.1 39.8 %collective-permute-start.13 = (bf16[96,768]{1,0:T(8,128)(2,1)S(1)}, bf16[96,768]{1,0:T(8,128)(2,1)}, u32[]{:S(2)}, u32[]{:S(2)}) collective-permute-start(bf16[96,768]{1,0:T(8,128)(2,1)S(1)} %copy-done.73), channel_id=1, source_target_pairs={{0,8},{1,9},{2,10},{3,11},{4,12},{5,13},{6,14},{7,15},{8,16},{9,17... | collective-permute-start | bytes 442376 | tf_op jit(solution)/shard_map/ppermute | solution.py:539
  81.3 109.3 %collective-permute-start.9 = (bf16[768,768]{1,0:T(8,128)(2,1)}, bf16[768,768]{1,0:T(8,128)(2,1)S(1)}, u32[]{:S(2)}, u32[]{:S(2)}) collective-permute-start(bf16[768,768]{1,0:T(8,128)(2,1)} %bitcast.106), channel_id=1, source_target_pairs={{0,2},{1,3},{2,0},{3,1},{4,6},{5,7},{6,4},{7,5},{8,10},{9,11},{10,... | collective-permute-start | bytes 3538952 | tf_op jit(solution)/shard_map/ppermute | solution.py:539
  100.0 45.1 %collective-permute-start.16 = (bf16[96,768]{1,0:T(8,128)(2,1)S(1)}, bf16[96,768]{1,0:T(8,128)(2,1)}, u32[]{:S(2)}, u32[]{:S(2)}) collective-permute-start(bf16[96,768]{1,0:T(8,128)(2,1)S(1)} %copy-done.73), channel_id=1, source_target_pairs={{0,4},{1,5},{2,6},{3,7},{4,0},{5,1},{6,2},{7,3},{8,12},{9,13},{10,... | collective-permute-start | bytes 442376 | tf_op jit(solution)/shard_map/ppermute | solution.py:539
  102.1 43.1 %collective-permute-start.17 = (bf16[96,768]{1,0:T(8,128)(2,1)}, bf16[96,768]{1,0:T(8,128)(2,1)}, u32[]{:S(2)}, u32[]{:S(2)}) collective-permute-start(bf16[96,768]{1,0:T(8,128)(2,1)} %collective-permute-done.13.refs_1_), channel_id=1, source_target_pairs={{0,4},{1,5},{2,6},{3,7},{4,0},{5,1},{6,2},{7,3},{8,12},{9,13},{10,... | collective-permute-start | bytes 442376 | tf_op jit(solution)/shard_map/ppermute | solution.py:539
  103.6 43.2 %collective-permute-start.18 = (bf16[96,768]{1,0:T(8,128)(2,1)}, bf16[96,768]{1,0:T(8,128)(2,1)}, u32[]{:S(2)}, u32[]{:S(2)}) collective-permute-start(bf16[96,768]{1,0:T(8,128)(2,1)} %collective-permute-done.14.refs_2_), channel_id=1, source_target_pairs={{0,4},{1,5},{2,6},{3,7},{4,0},{5,1},{6,2},{7,3},{8,12},{9,13},{10,... | collective-permute-start | bytes 442376 | tf_op jit(solution)/shard_map/ppermute | solution.py:539
  105.2 41.6 %collective-permute-start.19 = (bf16[96,768]{1,0:T(8,128)(2,1)}, bf16[96,768]{1,0:T(8,128)(2,1)}, u32[]{:S(2)}, u32[]{:S(2)}) collective-permute-start(bf16[96,768]{1,0:T(8,128)(2,1)} %collective-permute-done.15.refs_3_), channel_id=1, source_target_pairs={{0,4},{1,5},{2,6},{3,7},{4,0},{5,1},{6,2},{7,3},{8,12},{9,13},{10,... | collective-permute-start | bytes 442376 | tf_op jit(solution)/shard_map/ppermute | solution.py:539
  145.1 59.3 %collective-permute-start.7 = (bf16[768,768]{1,0:T(8,128)(2,1)S(1)}, bf16[768,768]{1,0:T(8,128)(2,1)S(1)}, u32[]{:S(2)}, u32[]{:S(2)}) collective-permute-start(bf16[768,768]{1,0:T(8,128)(2,1)S(1)} %bitcast.107), channel_id=1, source_target_pairs={{0,1},{1,0},{2,3},{3,2},{4,5},{5,4},{6,7},{7,6},{8,9},{9,8},{10,11... | collective-permute-start | bytes 3538952 | tf_op jit(solution)/shard_map/ppermute | solution.py:539
  145.2 59.4 %collective-permute-start.31 = (bf16[768,768]{1,0:T(8,128)(2,1)}, bf16[768,768]{1,0:T(8,128)(2,1)}, u32[]{:S(2)}, u32[]{:S(2)}) collective-permute-start(bf16[768,768]{1,0:T(8,128)(2,1)} %bitcast.112), channel_id=1, source_target_pairs={{0,2},{1,3},{2,0},{3,1},{4,6},{5,7},{6,4},{7,5},{8,10},{9,11},{10,... | collective-permute-start | bytes 3538952 | tf_op jit(solution)/shard_map/ppermute | solution.py:539
  184.4 28.4 %collective-permute-start.29 = (bf16[768,768]{1,0:T(8,128)(2,1)}, bf16[768,768]{1,0:T(8,128)(2,1)}, u32[]{:S(2)}, u32[]{:S(2)}) collective-permute-start(bf16[768,768]{1,0:T(8,128)(2,1)} %bitcast.116), channel_id=1, source_target_pairs={{0,2},{1,3},{2,0},{3,1},{4,6},{5,7},{6,4},{7,5},{8,10},{9,11},{10,... | collective-permute-start | bytes 3538952 | tf_op jit(solution)/shard_map/ppermute | solution.py:539
  190.6 66.1 %collective-permute-start.28 = (bf16[768,768]{1,0:T(8,128)(2,1)}, bf16[768,768]{1,0:T(8,128)(2,1)}, u32[]{:S(2)}, u32[]{:S(2)}) collective-permute-start(bf16[768,768]{1,0:T(8,128)(2,1)} %bitcast.113), channel_id=1, source_target_pairs={{0,1},{1,0},{2,3},{3,2},{4,5},{5,4},{6,7},{7,6},{8,9},{9,8},{10,11... | collective-permute-start | bytes 3538952 | tf_op jit(solution)/shard_map/ppermute | solution.py:539
  190.6 27.3 %collective-permute-start.11 = (bf16[768,768]{1,0:T(8,128)(2,1)S(1)}, bf16[768,768]{1,0:T(8,128)(2,1)S(1)}, u32[]{:S(2)}, u32[]{:S(2)}) collective-permute-start(bf16[768,768]{1,0:T(8,128)(2,1)S(1)} %collective-permute-done.9.w_ref.refs_6_), channel_id=1, source_target_pairs={{0,1},{1,0},{2,3},{3,2},{4,5},{5,4},{6,7},{7,6},{8,9},{9,8},{10,11... | collective-permute-start | bytes 3538952 | tf_op jit(solution)/shard_map/ppermute | solution.py:539
  204.5 52.2 %collective-permute-start.20 = (bf16[768,768]{1,0:T(8,128)(2,1)S(1)}, bf16[768,768]{1,0:T(8,128)(2,1)}, u32[]{:S(2)}, u32[]{:S(2)}) collective-permute-start(bf16[768,768]{1,0:T(8,128)(2,1)S(1)} %bitcast.117), channel_id=1, source_target_pairs={{0,1},{1,0},{2,3},{3,2},{4,5},{5,4},{6,7},{7,6},{8,9},{9,8},{10,11... | collective-permute-start | bytes 3538952 | tf_op jit(solution)/shard_map/ppermute | solution.py:539
  204.6 27.6 %collective-permute-start.32 = (bf16[768,768]{1,0:T(8,128)(2,1)}, bf16[768,768]{1,0:T(8,128)(2,1)S(1)}, u32[]{:S(2)}, u32[]{:S(2)}) collective-permute-start(bf16[768,768]{1,0:T(8,128)(2,1)} %collective-permute-done.31.refs_2_.refs_14_), channel_id=1, source_target_pairs={{0,1},{1,0},{2,3},{3,2},{4,5},{5,4},{6,7},{7,6},{8,9},{9,8},{10,11... | collective-permute-start | bytes 3538952 | tf_op jit(solution)/shard_map/ppermute | solution.py:539
  212.8 19.4 %collective-permute-start.30 = (bf16[768,768]{1,0:T(8,128)(2,1)}, bf16[768,768]{1,0:T(8,128)(2,1)S(1)}, u32[]{:S(2)}, u32[]{:S(2)}) collective-permute-start(bf16[768,768]{1,0:T(8,128)(2,1)} %collective-permute-done.29.refs_0_.refs_10_), channel_id=1, source_target_pairs={{0,1},{1,0},{2,3},{3,2},{4,5},{5,4},{6,7},{7,6},{8,9},{9,8},{10,11... | collective-permute-start | bytes 3538952 | tf_op jit(solution)/shard_map/ppermute | solution.py:539
  358.0 45.9 %collective-permute-start.53 = (bf16[8,96,768]{2,1,0:T(8,128)(2,1)}, bf16[8,96,768]{2,1,0:T(8,128)(2,1)}, u32[]{:S(2)}, u32[]{:S(2)}) collective-permute-start(bf16[8,96,768]{2,1,0:T(8,128)(2,1)} %get-tuple-element.135), channel_id=1, source_target_pairs={{0,1},{1,0},{2,3},{3,2},{4,5},{5,4},{6,7},{7,6},{8,9},{9,8},{10,11... | collective-permute-start | bytes 3538952 | tf_op jit(solution)/shard_map/ppermute | solution.py:539
  358.5 48.0 %collective-permute-start.46 = (bf16[8,96,768]{2,1,0:T(8,128)(2,1)}, bf16[8,96,768]{2,1,0:T(8,128)(2,1)}, u32[]{:S(2)}, u32[]{:S(2)}) collective-permute-start(bf16[8,96,768]{2,1,0:T(8,128)(2,1)} %get-tuple-element.131), channel_id=1, source_target_pairs={{0,1},{1,0},{2,3},{3,2},{4,5},{5,4},{6,7},{7,6},{8,9},{9,8},{10,11... | collective-permute-start | bytes 3538952 | tf_op jit(solution)/shard_map/ppermute | solution.py:539
  358.5 50.2 %collective-permute-start.34 = (bf16[8,96,768]{2,1,0:T(8,128)(2,1)}, bf16[8,96,768]{2,1,0:T(8,128)(2,1)}, u32[]{:S(2)}, u32[]{:S(2)}) collective-permute-start(bf16[8,96,768]{2,1,0:T(8,128)(2,1)} %get-tuple-element.113), channel_id=1, source_target_pairs={{0,1},{1,0},{2,3},{3,2},{4,5},{5,4},{6,7},{7,6},{8,9},{9,8},{10,11... | collective-permute-start | bytes 3538952 | tf_op jit(solution)/shard_map/ppermute | solution.py:539
  404.0 32.2 %collective-permute-start.33 = (bf16[8,96,768]{2,1,0:T(8,128)(2,1)}, bf16[8,96,768]{2,1,0:T(8,128)(2,1)S(1)}, u32[]{:S(2)}, u32[]{:S(2)}) collective-permute-start(bf16[8,96,768]{2,1,0:T(8,128)(2,1)} %copy-done.45), channel_id=1, source_target_pairs={{0,1},{1,0},{2,3},{3,2},{4,5},{5,4},{6,7},{7,6},{8,9},{9,8},{10,11... | collective-permute-start | bytes 3538952 | tf_op jit(solution)/shard_map/ppermute | solution.py:539
  406.5 28.9 %collective-permute-start.54 = (bf16[8,96,768]{2,1,0:T(8,128)(2,1)S(1)}, bf16[8,96,768]{2,1,0:T(8,128)(2,1)S(1)}, u32[]{:S(2)}, u32[]{:S(2)}) collective-permute-start(bf16[8,96,768]{2,1,0:T(8,128)(2,1)S(1)} %add_convert_fusion), channel_id=1, source_target_pairs={{0,2},{1,3},{2,0},{3,1},{4,6},{5,7},{6,4},{7,5},{8,10},{9,11},{10,... | collective-permute-start | bytes 3538952 | tf_op jit(solution)/shard_map/ppermute | solution.py:539
  408.8 51.9 %collective-permute-start.47 = (bf16[8,96,768]{2,1,0:T(8,128)(2,1)S(1)}, bf16[8,96,768]{2,1,0:T(8,128)(2,1)S(1)}, u32[]{:S(2)}, u32[]{:S(2)}) collective-permute-start(bf16[8,96,768]{2,1,0:T(8,128)(2,1)S(1)} %add_convert_fusion.2), channel_id=1, source_target_pairs={{0,2},{1,3},{2,0},{3,1},{4,6},{5,7},{6,4},{7,5},{8,10},{9,11},{10,... | collective-permute-start | bytes 3538952 | tf_op jit(solution)/shard_map/ppermute | solution.py:539
  412.1 73.0 %collective-permute-start.35 = (bf16[8,96,768]{2,1,0:T(8,128)(2,1)S(1)}, bf16[8,96,768]{2,1,0:T(8,128)(2,1)S(1)}, u32[]{:S(2)}, u32[]{:S(2)}) collective-permute-start(bf16[8,96,768]{2,1,0:T(8,128)(2,1)S(1)} %add_convert_fusion.4), channel_id=1, source_target_pairs={{0,2},{1,3},{2,0},{3,1},{4,6},{5,7},{6,4},{7,5},{8,10},{9,11},{10,... | collective-permute-start | bytes 3538952 | tf_op jit(solution)/shard_map/ppermute | solution.py:539
  435.6 50.2 %collective-permute-start.55 = (bf16[4,96,768]{2,1,0:T(8,128)(2,1)S(1)}, bf16[4,96,768]{2,1,0:T(8,128)(2,1)S(1)}, u32[]{:S(2)}, u32[]{:S(2)}) collective-permute-start(bf16[4,96,768]{2,1,0:T(8,128)(2,1)S(1)} %add_convert_fusion.7), channel_id=1, source_target_pairs={{0,4},{1,5},{2,6},{3,7},{4,0},{5,1},{6,2},{7,3},{8,12},{9,13},{10,... | collective-permute-start | bytes 1769480 | tf_op jit(solution)/shard_map/ppermute | solution.py:539
  460.9 27.3 %collective-permute-start.48 = (bf16[4,96,768]{2,1,0:T(8,128)(2,1)S(1)}, bf16[4,96,768]{2,1,0:T(8,128)(2,1)S(1)}, u32[]{:S(2)}, u32[]{:S(2)}) collective-permute-start(bf16[4,96,768]{2,1,0:T(8,128)(2,1)S(1)} %add_convert_fusion.10), channel_id=1, source_target_pairs={{0,4},{1,5},{2,6},{3,7},{4,0},{5,1},{6,2},{7,3},{8,12},{9,13},{10,... | collective-permute-start | bytes 1769480 | tf_op jit(solution)/shard_map/ppermute | solution.py:539
  486.0 15.9 %collective-permute-start.56 = (bf16[96,768]{1,0:T(8,128)(2,1)S(1)}, bf16[96,768]{1,0:T(8,128)(2,1)S(1)}, u32[]{:S(2)}, u32[]{:S(2)}) collective-permute-start(bf16[96,768]{1,0:T(8,128)(2,1)S(1)} %slice_bitcast_fusion), channel_id=1, source_target_pairs={{0,8},{1,9},{2,10},{3,11},{4,12},{5,13},{6,14},{7,15},{8,16},{9,17... | collective-permute-start | bytes 442376 | tf_op jit(solution)/shard_map/ppermute | solution.py:539
  (125 other events, 1188.9 us)

commit v2 on v1

v2 whole, which is shorter than its diff:
```python
import functools

import jax
import jax.numpy as jnp
from jax import lax
from jax.experimental import pallas as pl
from jax.experimental.pallas import tpu as pltpu
from jax.sharding import PartitionSpec as P

HEAD_DIM = 64
SEQ_LEN = 512
HALF = 256
EPS = 1e-05
AXES = ("fsdp", "tp")
BF = jnp.bfloat16
F32 = jnp.float32
MB = 1 << 20
SHARE = 0.3
BIAS_OUT, GAIN_ATTN, SHIFT_ATTN, GAIN_MLP, SHIFT_MLP, BIAS_DOWN = (slice(i, i + 1) for i in range(6))
VMEM_MB = 36
SMALL_ATTN = 768


def dot(left, right):
    return lax.dot_general(left, right, (((1,), (0,)), ((), ())), preferred_element_type=F32)


def dot_nt(left, right):
    return lax.dot_general(left, right, (((1,), (1,)), ((), ())), preferred_element_type=F32)


def dot_tn(left, right):
    return lax.dot_general(left, right, (((0,), (0,)), ((), ())), preferred_element_type=F32)


def whole(shape):
    zeros = (0,) * len(shape)
    return pl.BlockSpec(shape, lambda *_: zeros)


def params(limit_mb):
    return pltpu.CompilerParams(vmem_limit_bytes=(VMEM_MB or limit_mb) * MB)


def cost(flops, nbytes, trans=0):
    return pl.CostEstimate(
        flops=int(flops * SHARE), bytes_accessed=int(nbytes * SHARE), transcendentals=int(trans * SHARE)
    )


def unit_rows(rows):
    centre = rows - jnp.mean(rows, axis=-1, keepdims=True)
    spread = lax.rsqrt(jnp.mean(centre * centre, axis=-1, keepdims=True) + EPS)
    return centre * spread, spread


def norm_back(grad_out, unit, spread, gain):
    scaled = grad_out * gain
    inner = jnp.mean(scaled * unit, axis=-1, keepdims=True)
    return spread * (scaled - jnp.mean(scaled, axis=-1, keepdims=True) - unit * inner)


def add_sum(ref, value):
    @pl.when(pl.program_id(0) == 0)
    def _():
        ref[...] = jnp.zeros_like(ref)

    ref[...] += jnp.sum(value, axis=0, keepdims=True)


def start_kernel(x_ref, cot_ref, qv_ref, up_ref, *refs):
    vectors, (n1_ref, sum_ref, small_ref, table_ref) = refs[:6], refs[6:]

    @pl.when(pl.program_id(0) == 0)
    def _():
        for i, ref in enumerate(vectors):
            table_ref[i : i + 1] = ref[...].astype(F32).reshape(1, -1)
        small_ref[...] = jnp.zeros_like(small_ref)
        for c in range(2):
            pair, lone = (0, 384) if c == 0 else (256, 448)
            row = qv_ref[c : c + 1].astype(F32)
            small_ref[:, pair : pair + 128] = row[:, 0:128]
            small_ref[:, lone : lone + HEAD_DIM] = row[:, 128:192]
        small_ref[:, SMALL_ATTN:] = up_ref[...].astype(F32).reshape(1, -1)

    unit, _ = unit_rows(x_ref[...].astype(F32))
    normed = unit * table_ref[GAIN_ATTN] + table_ref[SHIFT_ATTN]
    n1_ref[...] = normed.astype(BF)
    add_sum(sum_ref, cot_ref[...].astype(F32))


def start_call(x, cot, bias_qv, bias_up, vectors):
    rows, d = x.shape
    units = bias_up.shape[0]
    tile = 256
    by_rows = pl.BlockSpec((tile, d), lambda i: (i, 0))
    return pl.pallas_call(
        start_kernel,
        grid=(rows // tile,),
        in_specs=[by_rows, by_rows, whole(bias_qv.shape), whole(bias_up.shape)]
        + [whole(v.shape) for v in vectors],
        out_specs=[by_rows]
        + [whole((1, d)), whole((1, SMALL_ATTN + units)), whole((8, d))],
        out_shape=[
            jax.ShapeDtypeStruct((rows, d), BF),
            jax.ShapeDtypeStruct((1, d), F32),
            jax.ShapeDtypeStruct((1, SMALL_ATTN + units), F32),
            jax.ShapeDtypeStruct((8, d), F32),
        ],
        compiler_params=params(24),
        cost_estimate=cost(0, 10 * rows * d),
        name="start",
    )(x, cot, bias_qv, bias_up, *vectors)


def assemble_kernel(count, place_ref, *refs):
    pieces, out_ref = refs[: 2 * count], refs[2 * count]
    z, x = place_ref[0], place_ref[1]
    for k in range(count):
        for dx in range(2):
            piece = pieces[dx * count + k]
            size = piece.shape[-2]
            slot = lax.rem(z - k + count, count) * 2 + lax.rem(x + dx, 2)
            value = piece[...].reshape(size, piece.shape[-1])
            out_ref[pl.ds(pl.multiple_of(slot * size, size), size)] = value


def assemble(place, pieces):
    count = len(pieces) // 2
    rows, cols = pieces[0][0].shape[-2:]
    specs = []
    for array, lead in pieces:
        block = (1,) * len(lead) + (rows, cols)
        specs.append(pl.BlockSpec(block, lambda *_, lead=lead: lead + (0, 0)))
    return pl.pallas_call(
        functools.partial(assemble_kernel, count),
        grid=(1,),
        in_specs=[pl.BlockSpec(memory_space=pltpu.SMEM)]
        + specs,
        out_specs=whole((2 * count * rows, cols)),
        out_shape=jax.ShapeDtypeStruct((2 * count * rows, cols), BF),
        compiler_params=params(16),
        cost_estimate=cost(0, 8 * count * rows * cols),
        name="assemble",
    )(place, *[array for array, _ in pieces])


HEAD_PLACES = ((0, 1, 2, 0, 0), (0, 1, 2, 64, 64), (3, 4, 3, 0, 64))


def lane_keep(tile, first):
    lanes = lax.broadcasted_iota(jnp.int32, tile.shape, 1)
    keep = (lanes >= first) & (lanes < first + HEAD_DIM)
    return jnp.where(keep, tile, jnp.zeros_like(tile))


def score_block(keys, query, start, stop, first_query):
    scores = dot_nt(keys[start:stop], query)
    if stop - 1 > first_query:
        key_idx = lax.broadcasted_iota(jnp.int32, scores.shape, 0) + start
        query_idx = lax.broadcasted_iota(jnp.int32, scores.shape, 1) + first_query
        scores = jnp.where(key_idx <= query_idx, scores, -1e30)
    return scores


def attend_kernel(n1_ref, w_ref, bias_ref, proj_ref, mixed_ref, lse_ref):
    projected = (dot(n1_ref[...], w_ref[...]) + bias_ref[...].astype(F32)).astype(BF)
    proj_ref[...] = projected
    lse_ref[...] = jnp.zeros_like(lse_ref)
    outs = {}
    for head, (qt, kt, vt, qk_lane, v_lane) in enumerate(HEAD_PLACES):
        query = lane_keep(projected[:, qt * 128 : qt * 128 + 128], qk_lane) * BF(0.125)
        keys = projected[:, kt * 128 : kt * 128 + 128]
        values = projected[:, vt * 128 : vt * 128 + 128]
        for block in range(2):
            first = block * HALF
            last = first + HALF
            scores = score_block(keys, query[first:last], 0, last, first)
            top = jnp.max(scores, axis=0, keepdims=True)
            weight = jnp.exp(scores - top)
            total = jnp.sum(weight, axis=0, keepdims=True)
            mixed = dot_tn(values[0:last], weight.astype(BF)) * (1.0 / total)
            outs[head, block] = mixed[v_lane : v_lane + HEAD_DIM]
            lse_ref[0, head : head + 1, first:last] = top + jnp.log(total)
    for block in range(2):
        first = block * HALF
        rows = slice(first, first + HALF)
        single = jnp.concatenate([jnp.zeros_like(outs[2, block]), outs[2, block]], axis=0)
        pair = jnp.concatenate([outs[0, block], outs[1, block]], axis=0)
        mixed_ref[rows, 0:128] = single.T.astype(BF)
        mixed_ref[rows, 128:256] = pair.T.astype(BF)


def attend_call(n1, w, bias):
    rows, d = n1.shape
    seqs = rows // SEQ_LEN
    return pl.pallas_call(
        attend_kernel,
        grid=(seqs,),
        in_specs=[
            pl.BlockSpec((SEQ_LEN, d), lambda i: (i, 0)),
            pl.BlockSpec((d, 640), lambda i: (0, 0)),
            pl.BlockSpec((1, 640), lambda i: (0, 0)),
        ],
        out_specs=[
            pl.BlockSpec((SEQ_LEN, 640), lambda i: (i, 0)),
            pl.BlockSpec((SEQ_LEN, 256), lambda i: (i, 0)),
            pl.BlockSpec((1, 8, SEQ_LEN), lambda i: (i, 0, 0)),
        ],
        out_shape=[
            jax.ShapeDtypeStruct((rows, 640), BF),
            jax.ShapeDtypeStruct((rows, 256), BF),
            jax.ShapeDtypeStruct((seqs, 8, SEQ_LEN), F32),
        ],
        compiler_params=params(32),
        cost_estimate=cost(6e9, 8e6),
        name="attend",
    )(n1, w, bias)


def middle_kernel(x_ref, table_ref, *refs):
    mixed, weights, (mid_ref, n2_ref) = refs[0:4], refs[4:8], refs[8:]
    attended = table_ref[BIAS_OUT]
    for m, w in zip(mixed, weights):
        attended = attended + dot_nt(m[...], w[...])
    middle = x_ref[...].astype(F32) + attended
    mid_ref[...] = middle
    unit, _ = unit_rows(middle)
    normed = unit * table_ref[GAIN_MLP] + table_ref[SHIFT_MLP]
    n2_ref[...] = normed.astype(BF)


def middle_call(x, table, mixed, weights):
    rows, d = x.shape
    tile = 256
    by_rows = pl.BlockSpec((tile, d), lambda i: (i, 0))
    return pl.pallas_call(
        middle_kernel,
        grid=(rows // tile,),
        in_specs=[by_rows, whole(table.shape)]
        + [pl.BlockSpec((tile, 256), lambda i: (i, 0))] * 4
        + [pl.BlockSpec((d, 256), lambda i: (0, 2))] * 4,
        out_specs=[by_rows, by_rows],
        out_shape=[
            jax.ShapeDtypeStruct((rows, d), F32),
            jax.ShapeDtypeStruct((rows, d), BF),
        ],
        compiler_params=params(24),
        cost_estimate=cost(2 * rows * d * 1024, 16e6),
        name="middle",
    )(x, table, *mixed, *weights)


def gelu_both(value):
    cumulative = 0.5 + 0.5 * lax.erf(value * 2.0**-0.5)
    bell = jnp.exp(-0.5 * value * value)
    return value * cumulative, cumulative + value * bell * (2.0 * 3.141592653589793) ** -0.5


def store_all(ref, lead, place_ref, value, count, got_ref=None, got_lead=()):
    z, x = place_ref[0], place_ref[1]
    size = value.shape[0] // (2 * count)
    for block in range(2 * count):
        slot = lax.rem(x + block % 2, 2) * count + lax.rem(block // 2 - z + count, count)
        part = value[block * size : (block + 1) * size]
        if got_ref is not None:
            part = part + got_ref[got_lead + (slot,)].astype(F32)
        ref[lead + (slot,)] = part.astype(BF)


def store_split(home_ref, away_ref, got_ref, lead, place_ref, value, count):
    z, x = place_ref[0], place_ref[1]
    size = value.shape[0] // (2 * count)
    for pair in range(count):
        slot = lax.rem(pair - z + count, count)
        first = value[2 * pair * size : (2 * pair + 1) * size]
        second = value[(2 * pair + 1) * size : (2 * pair + 2) * size]
        home = jnp.where(x == 0, first, second) + got_ref[lead + (slot,)].astype(F32)
        away = jnp.where(x == 0, second, first) + got_ref[lead + (count + slot,)].astype(F32)
        home_ref[slot] = home.astype(BF)
        away_ref[slot] = away.astype(BF)


def feed_kernel(count, tokens, has_got, place_ref, n2_ref, cot_ref, *refs):
    up_ref, down_ref, bias_ref = refs[0:3]
    got_ref = refs[3] if has_got else None
    outs = refs[3 + has_got :]
    hidden_ref, pre_ref, sum_ref = outs[0:3]
    rows = n2_ref.shape[0]
    up, down, bias = up_ref[...], down_ref[...], bias_ref[...].astype(F32)
    total = jnp.zeros_like(bias)
    for first in range(0, rows, tokens):
        here = slice(first, first + tokens)
        pre = dot(n2_ref[here], up) + bias
        grad_hidden = dot(cot_ref[here], down)
        hidden, slope = gelu_both(pre)
        hidden_ref[here] = hidden.astype(BF)
        grad_pre = (grad_hidden * slope).astype(BF)
        pre_ref[here] = grad_pre
        total = total + jnp.sum(grad_pre.astype(F32), axis=0, keepdims=True)
    sum_ref[...] = total
    grads = (dot_tn(n2_ref[...], pre_ref[...]), dot_tn(cot_ref[...], hidden_ref[...]))
    if has_got:
        store_split(outs[3], outs[4], got_ref, (0,), place_ref, grads[0], count)
        store_all(outs[5], (), place_ref, grads[1], count, got_ref, (1,))
    else:
        store_all(outs[3], (0,), place_ref, grads[0], count)
        store_all(outs[3], (1,), place_ref, grads[1], count)


def feed_call(place, count, n2, cot, up, down, small, got=None):
    rows, d = n2.shape
    units = up.shape[1]
    tile = 256
    shard = d // (2 * count)
    cols = lambda n: pl.BlockSpec((n, tile), lambda i: (0, i))
    hid = jax.ShapeDtypeStruct((rows, units), BF)
    both_spec = pl.BlockSpec((2, 2 * count, shard, tile), lambda i: (0, 0, 0, i))
    if got is None:
        grad_specs = [both_spec]
        grads = [jax.ShapeDtypeStruct((2, 2 * count, shard, units), BF)]
    else:
        grad_specs = [pl.BlockSpec((n, shard, tile), lambda i: (0, 0, i)) for n in (count, count, 2 * count)]
        grads = [jax.ShapeDtypeStruct((n, shard, units), BF) for n in (count, count, 2 * count)]
    gots = () if got is None else (got,)
    return pl.pallas_call(
        functools.partial(feed_kernel, count, 512, len(gots)),
        grid=(units // tile,),
        in_specs=[
            pl.BlockSpec(memory_space=pltpu.SMEM),
            whole((rows, d)),
            whole((rows, d)),
            cols(d),
            cols(d),
            pl.BlockSpec((1, tile), lambda i: (0, SMALL_ATTN // tile + i)),
        ]
        + [both_spec] * len(gots),
        out_specs=[cols(rows)] * 2 + [cols(1)] + grad_specs,
        out_shape=[hid] * 2 + [jax.ShapeDtypeStruct((1, units), F32)] + grads,
        compiler_params=params(40),
        cost_estimate=cost(2 * 4 * rows * d * units, 16e6, rows * units),
        name="feed",
    )(place, n2, cot, up, down, small, *gots)


def turn_kernel(_, mid_ref, cot_ref, table_ref, *refs):
    pre, ups = refs[0:4], refs[4:8]
    gmid_ref, grows_ref, gain_sum, shift_sum, bias_sum = refs[-5:]
    grad = None
    for g, w in zip(pre, ups):
        term = dot_nt(g[...], w[...])
        grad = term if grad is None else grad + term
    unit, spread = unit_rows(mid_ref[...])
    add_sum(gain_sum, grad * unit)
    add_sum(shift_sum, grad)
    back = norm_back(grad, unit, spread, table_ref[GAIN_MLP])
    grad_middle = cot_ref[...].astype(F32) + back
    gmid_ref[...] = grad_middle
    rows = grad_middle.astype(BF)
    grows_ref[...] = rows
    add_sum(bias_sum, rows.astype(F32))


def turn_call(place, middle, cot, table, pre, ups):
    rows, d = middle.shape
    units = ups[0].shape[1]
    tile = 256
    by_rows = pl.BlockSpec((tile, d), lambda i: (i, 0))
    kept = pl.BlockSpec((d, units), lambda i: (0, 0), pipeline_mode=pl.Buffered(1))
    total = jax.ShapeDtypeStruct((1, d), F32)
    return pl.pallas_call(
        turn_kernel,
        grid=(rows // tile,),
        in_specs=[pl.BlockSpec(memory_space=pltpu.SMEM), by_rows, by_rows, whole(table.shape)]
        + [pl.BlockSpec((tile, units), lambda i: (i, 0))] * 4
        + [kept] * 4,
        out_specs=[by_rows] * 2 + [whole((1, d))] * 3,
        out_shape=[
            jax.ShapeDtypeStruct((rows, d), F32),
            jax.ShapeDtypeStruct((rows, d), BF),
            total,
            total,
            total,
        ],
        compiler_params=params(32),
        cost_estimate=cost(2 * 4 * rows * d * units, 20e6),
        name="turn",
    )(place, middle, cot, table, *pre, *ups)


def output_kernel(_, mid_ref, table_ref, *refs):
    hidden, downs, out_ref = refs[0:4], refs[4:8], refs[-1]
    mlp = table_ref[BIAS_DOWN]
    for h, w in zip(hidden, downs):
        mlp = mlp + dot_nt(h[...], w[...])
    out_ref[...] = (mid_ref[...] + mlp).astype(BF)


def output_call(place, middle, table, hidden, downs):
    rows, d = middle.shape
    units = downs[0].shape[1]
    tile = 256
    by_rows = pl.BlockSpec((tile, d), lambda i: (i, 0))
    kept = pl.BlockSpec((d, units), lambda i: (0, 0), pipeline_mode=pl.Buffered(1))
    return pl.pallas_call(
        output_kernel,
        grid=(rows // tile,),
        in_specs=[pl.BlockSpec(memory_space=pltpu.SMEM), by_rows, whole(table.shape)]
        + [pl.BlockSpec((tile, units), lambda i: (i, 0))] * 4
        + [kept] * 4,
        out_specs=by_rows,
        out_shape=jax.ShapeDtypeStruct((rows, d), BF),
        compiler_params=params(32),
        cost_estimate=cost(2 * 4 * rows * d * units, 16e6),
        name="output",
    )(place, middle, table, *hidden, *downs)


def attend_back_kernel(
    count,
    has_got,
    place_ref,
    grows_ref,
    n1_ref,
    w_ref,
    proj_ref,
    mixed_ref,
    lse_ref,
    *refs,
):
    got_ref = refs[0] if has_got else None
    total = refs[-1]
    gproj_ref, sum_ref, *grad_refs = refs[-5:-1] if has_got else refs[-4:-1]
    step = pl.program_id(0)
    projected = proj_ref[...]
    grad_mixed = dot(grows_ref[...], w_ref[...]).astype(BF)
    parts = {}
    early = lax.broadcasted_iota(jnp.int32, (HALF, HALF), 0) <= lax.broadcasted_iota(jnp.int32, (HALF, HALF), 1)
    jobs = []
    for head, (qt, kt, vt, qk_lane, v_lane) in enumerate(HEAD_PLACES):
        mt = 0 if head == 2 else 1
        query = lane_keep(projected[:, qt * 128 : qt * 128 + 128], qk_lane) * BF(0.125)
        keys = projected[:, kt * 128 : kt * 128 + 128]
        values = projected[:, vt * 128 : vt * 128 + 128]
        grads = lane_keep(grad_mixed[:, mt * 128 : mt * 128 + 128], v_lane)
        parts["k", head] = [None, None]
        parts["v", head] = [None, None]
        for block in range(2):
            rows = slice(block * HALF, block * HALF + HALF)
            jobs.append((head, block, qk_lane, query[rows], keys, values, grads[rows]))

    def first_stage(job):
        head, block, _, qb, keys, values, gb = job
        last = block * HALF + HALF
        return dot_nt(keys[0:last], qb), dot_nt(values[0:last], gb)

    def last_stage(job, scores, gprobs):
        head, block, qk_lane, qb, keys, values, gb = job
        last = block * HALF + HALF
        lse = lse_ref[0, head : head + 1, last - HALF : last]
        probs = jnp.exp(scores - lse)
        corner = jnp.where(early, probs[last - HALF :], 0.0)
        probs = jnp.concatenate([probs[: last - HALF], corner], axis=0) if block else corner
        both = probs * gprobs
        delta = jnp.sum(both, axis=0, keepdims=True)
        gscores = (both - probs * delta).astype(BF)
        gq = dot_tn(keys[0:last], gscores) * 0.125
        parts["q", head, block] = gq[qk_lane : qk_lane + HEAD_DIM]
        gk = dot(gscores, qb)
        gv = dot(probs.astype(BF), gb)
        for name, got in (("k", gk), ("v", gv)):
            held = parts[name, head]
            for b in range(block + 1):
                part = got[b * HALF : b * HALF + HALF]
                held[b] = part if held[b] is None else held[b] + part

    waiting = None
    for job in jobs + [None]:
        ahead = None if job is None else (job, *first_stage(job))
        if waiting is not None:
            last_stage(*waiting)
        waiting = ahead
    for block in range(2):
        rows = slice(block * HALF, block * HALF + HALF)
        pair = jnp.concatenate([parts["q", 0, block], parts["q", 1, block]], axis=0).T
        lone = parts["q", 2, block]
        lone = jnp.concatenate([lone, jnp.zeros_like(lone)], axis=0).T
        gproj_ref[rows, 0:128] = pair.astype(BF)
        gproj_ref[rows, 128:256] = (parts["k", 0][block] + parts["k", 1][block]).astype(BF)
        gproj_ref[rows, 256:384] = (parts["v", 0][block] + parts["v", 1][block]).astype(BF)
        gproj_ref[rows, 384:512] = (lone + parts["v", 2][block]).astype(BF)
        gproj_ref[rows, 512:640] = parts["k", 2][block].astype(BF)
    gproj = gproj_ref[...]
    add_sum(sum_ref, gproj.astype(F32))
    grad_a = dot_tn(n1_ref[...], gproj)
    grad_b = dot_tn(grows_ref[...], mixed_ref[...])
    grad = jnp.concatenate(
        [grad_a[:, 0:512], grad_a[:, 512:640] + grad_b[:, 0:128], grad_b[:, 128:256]], axis=1
    )

    @pl.when(step == 0)
    def _():
        total[...] = grad

    @pl.when(step > 0)
    def _():
        total[...] += grad

    @pl.when(step == pl.num_programs(0) - 1)
    def _():
        if has_got:
            store_split(*grad_refs, got_ref, (), place_ref, total[...], count)
        else:
            store_all(*grad_refs, (), place_ref, total[...], count)


def attend_back_call(place, count, grows, n1, w, proj, mixed, lse, got=None):
    rows, d = grows.shape
    seqs = rows // SEQ_LEN
    shard = d // (2 * count)
    by_rows = lambda n: pl.BlockSpec((SEQ_LEN, n), lambda i: (i, 0))
    gots = () if got is None else (got,)
    both = (2 * count, shard, 768)
    grads = [both] if got is None else [(count, shard, 768)] * 2
    return pl.pallas_call(
        functools.partial(attend_back_kernel, count, len(gots)),
        grid=(seqs,),
        in_specs=[
            pl.BlockSpec(memory_space=pltpu.SMEM),
            by_rows(d),
            by_rows(d),
            pl.BlockSpec((d, 256), lambda i: (0, 2)),
            by_rows(640),
            by_rows(256),
            pl.BlockSpec((1, 8, SEQ_LEN), lambda i: (i, 0, 0)),
        ]
        + [whole(both)] * len(gots),
        out_specs=[by_rows(640), whole((1, 640))] + [whole(g) for g in grads],
        out_shape=[jax.ShapeDtypeStruct((rows, 640), BF), jax.ShapeDtypeStruct((1, 640), F32)]
        + [jax.ShapeDtypeStruct(g, BF) for g in grads],
        scratch_shapes=[pltpu.VMEM((d, 768), F32)],
        compiler_params=params(40),
        cost_estimate=cost(10e9, 12e6),
        name="attend_back",
    )(place, grows, n1, w, proj, mixed, lse, *gots)


def finish_kernel(_, x_ref, gmid_ref, table_ref, *refs):
    gproj, weights, known, sum_proj, sum_up = refs[0:4], refs[4:8], refs[8:12], refs[12:16], refs[16:20]
    out_ref, keep_ref, away_ref, gain_sum, shift_sum = refs[20:]
    grad = None
    for g, w in zip(gproj, weights):
        term = dot_nt(g[...], w[...])
        grad = term if grad is None else grad + term
    unit, spread = unit_rows(x_ref[...].astype(F32))
    add_sum(gain_sum, grad * unit)
    add_sum(shift_sum, grad)
    back = norm_back(grad, unit, spread, table_ref[GAIN_ATTN])
    out_ref[...] = (gmid_ref[...] + back).astype(BF)

    @pl.when(pl.program_id(0) == pl.num_programs(0) - 1)
    def _():
        shared = jnp.concatenate(
            [r[...] for r in known] + [gain_sum[...], shift_sum[...]], axis=1
        )
        for dy in range(2):
            for dc, ref in enumerate((keep_ref, away_ref)):
                row = jnp.concatenate([shared, sum_proj[2 * dy + dc][...], sum_up[2 * dy + dc][...]], axis=1)
                ref[dy : dy + 1] = row


def finish_call(place, x, gmid, table, gproj, weights, known, sum_proj, sum_up):
    rows, d = x.shape
    tile = 256
    by_rows = pl.BlockSpec((tile, d), lambda i: (i, 0))
    width = 6 * d + sum_proj[0].shape[1] + sum_up[0].shape[1]
    return pl.pallas_call(
        finish_kernel,
        grid=(rows // tile,),
        in_specs=[pl.BlockSpec(memory_space=pltpu.SMEM), by_rows, by_rows, whole(table.shape)]
        + [pl.BlockSpec((tile, 640), lambda i: (i, 0))] * 4
        + [pl.BlockSpec((d, 640), lambda i: (0, 0))] * 4
        + [whole(v.shape) for v in (*known, *sum_proj, *sum_up)],
        out_specs=[by_rows, whole((2, width)), whole((2, width))],
        out_shape=[jax.ShapeDtypeStruct((rows, d), BF)] + [jax.ShapeDtypeStruct((2, width), F32)] * 2,
        scratch_shapes=[pltpu.VMEM((1, d), F32)] * 2,
        compiler_params=params(32),
        cost_estimate=cost(2 * 4 * rows * d * 640, 16e6),
        name="finish",
    )(place, x, gmid, table, *gproj, *weights, *known, *sum_proj, *sum_up)


class Links:
    def __init__(self, mesh):
        self.count = mesh.shape["fsdp"] // 2
        places = [
            (z, x, y, c)
            for z in range(self.count)
            for x in range(2)
            for y in range(2)
            for c in range(2)
        ]

        def index(z, x, y, c):
            return ((z * 2 + x) * 2 + y) * 2 + c

        def pairs(move):
            return [(index(*p), index(*move(*p))) for p in places]

        self.core = pairs(lambda z, x, y, c: (z, x, y, 1 - c))
        self.y = pairs(lambda z, x, y, c: (z, x, 1 - y, c))
        self.x = pairs(lambda z, x, y, c: (z, 1 - x, y, c))
        self.ring = pairs(lambda z, x, y, c: ((z + 1) % self.count, x, y, c))
        self.far = [
            pairs(lambda z, x, y, c, k=k: ((z + k) % self.count, x, y, c)) for k in range(self.count)
        ]
        self.back = [
            pairs(lambda z, x, y, c, k=k: ((z - k) % self.count, x, y, c)) for k in range(self.count)
        ]
        self.xy = pairs(lambda z, x, y, c: (z, 1 - x, 1 - y, c))
        self.trees = []
        step = 1
        while step < self.count:
            size = 4 if step * 4 <= self.count else 2
            self.trees.append(
                [pairs(lambda z, x, y, c, b=step * k: (z ^ b, x, y, c)) for k in range(1, size)]
            )
            step *= size

    @staticmethod
    def send(value, pairs):
        return lax.ppermute(value, AXES, pairs)


def plus(*terms, kind=BF):
    total = terms[0].astype(F32)
    for term in terms[1:]:
        total = total + term.astype(F32)
    return total.astype(kind)


def tie(value, *others):
    return lax.optimization_barrier((value, others))[0]


def ring_from(links, first):
    held = [first]
    for _ in range(links.count - 1):
        held.append(links.send(held[-1], links.ring))
    return held


def gather_and_attend(links, place, attn, up, down, n1, smalls):
    n = links.count
    half = n // 2

    near, lines, others, quads = [attn], [], [], []
    pair = jnp.stack([up, links.send(up, links.x)])
    steps = [jnp.stack([pair, links.send(tie(pair, n1), links.y)])]
    for k in range(1, n):
        before = ()
        if k == 2:
            before = (n1, pair)
        if k == half + 1:
            before += (others[0], smalls[2], steps[0])
        near.append(links.send(tie(near[-1], *before) if before else near[-1], links.ring))
        if (k + 1) % half == 0:
            lines.append(jnp.stack(near[-half:]))
            others.append(links.send(lines[-1], links.x))
            quads.append(links.send(jnp.stack([lines[-1], others[-1]]), links.y))
    steps.append(links.send(steps[0], links.ring))
    line = jnp.stack([down] + [links.send(down, links.far[k]) for k in range(1, n)])

    own = assemble(place, [(v[k // half], (k % half,)) for v in (lines, others) for k in range(n)])
    attn_w = [own, links.send(own, links.core)]
    proj, mixed, lse = [], [], []

    def attend(j, *before):
        p, m, s = attend_call(n1, attn_w[j], tie(smalls[j], *before) if before else smalls[j])
        proj.append(p)
        mixed.append(m)
        lse.append(s)

    attend(0)
    steps.append(links.send(tie(steps[1], mixed[0]), links.ring))
    line = tie(line, others[1], smalls[1], smalls[3])
    other = links.send(line, links.x)
    beyond = [links.send(tie(v, quads[1]), links.y) for v in (line, other)]
    attend(1, mixed[0])
    own = assemble(tie(place, mixed[1]), [(quads[k // half], (dx, k % half)) for dx in range(2) for k in range(n)])
    attn_w += [own, links.send(own, links.core)]
    attend(2, mixed[1], steps[2])
    for k in range(2, n - 1):
        steps.append(links.send(tie(steps[-1], mixed[1], other), links.ring))
    attend(3, mixed[2])

    last = tie(place, mixed[3])
    up_w, down_w = [], []
    for dy in range(2):
        own = assemble(last, [(v, (dy, dx)) for dx in range(2) for v in steps])
        up_w += [own, links.send(own, links.core)]
        own = assemble(last, [(v, (k,)) for v in ((line, other), beyond)[dy] for k in range(n)])
        down_w += [own, links.send(own, links.core)]
    return attn_w, up_w, down_w, proj, mixed, lse


def spread_sum(links, home):
    got = [links.send(home[k], links.far[k]) for k in range(1, links.count)]
    return plus(home[0], *got, kind=F32)


def sum_all(links, keep, away):
    rows = keep + links.send(away, links.core)
    near, far = rows[0:1], rows[1:2]
    total = (near + links.send(near, links.x)) + (
        links.send(far, links.y) + links.send(far, links.xy)
    )
    for pairs in links.trees:
        got = [total] + [links.send(total, p) for p in pairs]
        while len(got) > 1:
            got = [got[i] + got[i + 1] for i in range(0, len(got), 2)]
        total = got[0]
    return total


def pack_attn(w_qkv, w_out):
    q, k, v, o = w_qkv[:, 0], w_qkv[:, 1], w_qkv[:, 2], w_out.T
    return jnp.concatenate(
        [q[:, :128], k[:, :128], v[:, :128], q[:, 128:], v[:, 128:], k[:, 128:], o[:, 128:], o[:, :128]],
        axis=1,
    )


def unpack_attn(g):
    q = jnp.concatenate([g[:, 0:128], g[:, 384:448]], axis=1)
    k = jnp.concatenate([g[:, 128:256], g[:, 512:576]], axis=1)
    v = jnp.concatenate([g[:, 256:384], g[:, 448:512]], axis=1)
    o = jnp.concatenate([g[:, 640:768], g[:, 576:640]], axis=1)
    return jnp.stack([q, k, v], axis=1), o.T


def body(
    links,
    layer_input,
    w_qkv,
    bias_qv,
    w_out,
    bias_out,
    gain_attn,
    shift_attn,
    gain_mlp,
    shift_mlp,
    w_up,
    bias_up,
    w_down,
    bias_down,
    cotangent,
):
    fsdp = lax.axis_index("fsdp")
    place = jnp.stack([fsdp // 2, fsdp % 2]).astype(jnp.int32)
    count = links.count
    n1, sum_down, small, table = start_call(
        layer_input,
        cotangent,
        bias_qv,
        bias_up,
        (bias_out, gain_attn, shift_attn, gain_mlp, shift_mlp, bias_down),
    )
    small_y = links.send(small, links.y)
    smalls = [small, links.send(small, links.core), small_y, links.send(small_y, links.core)]
    attn_w, up_w, down_w, proj, mixed, lse = gather_and_attend(
        links, place, pack_attn(w_qkv, w_out), w_up, w_down.T, n1, smalls
    )

    middle, n2 = middle_call(tie(layer_input, up_w[0], up_w[2]), table, mixed, attn_w)

    hidden, pre, sum_up = [None] * 4, [None] * 4, [None] * 4
    up_home, up_away, down_sum = [None] * 2, [None] * 2, [None] * 2
    gots = [None] * 4
    for j in (1, 3, 0, 2):
        out = feed_call(
            place, count, n2, cotangent, up_w[j], down_w[j], smalls[j], gots[j]
        )
        hidden[j], pre[j], sum_up[j] = out[0:3]
        if j % 2:
            gots[j - 1] = links.send(out[3], links.core)
        else:
            up_home[j // 2], up_away[j // 2], down_sum[j // 2] = out[3:6]

    got_x0 = links.send(up_away[0], links.x)
    got_x1 = links.send(up_away[1], links.x)
    got_down = links.send(down_sum[1], links.y)
    gmid, grows, gain_two, shift_two, sum_out = turn_call(
        place, middle, cotangent, table, pre, up_w
    )

    gproj, sum_proj = [None] * 4, [None] * 4
    attn_home, attn_away = [None] * 2, [None] * 2

    def back(j, got, *before):
        out = attend_back_call(
            tie(place, *before) if before else place,
            count,
            grows,
            n1,
            attn_w[j],
            proj[j],
            mixed[j],
            lse[j],
            got,
        )
        gproj[j], sum_proj[j] = out[0:2]
        if j % 2:
            return links.send(out[2], links.core)
        attn_home[j // 2], attn_away[j // 2] = out[2:4]

    got_three = back(3, None, got_x0)
    up_beyond = plus(up_home[1], got_x1)
    got_up = links.send(up_beyond, links.y)
    got_one = back(1, None, up_beyond)
    down_away = plus(down_sum[0][count:], got_down[count:])
    got_x = links.send(down_away, links.x)
    back(2, got_three, down_away)
    got_a1 = links.send(attn_away[1], links.x)
    up_all = plus(up_home[0], got_x0, got_up)
    back(0, got_one, up_all, sum_proj[2])
    grad_up = spread_sum(links, up_all)
    got_a0 = links.send(attn_away[0], links.x)
    attn_beyond = plus(attn_home[1], got_a1)
    got_attn = links.send(attn_beyond, links.y)
    down_all = plus(down_sum[0][:count], got_down[:count], got_x)
    grad_down = spread_sum(links, down_all)
    grad_input, keep, away = finish_call(
        tie(place, attn_beyond, down_all),
        layer_input,
        gmid,
        table,
        gproj,
        attn_w,
        (sum_out, sum_down, gain_two, shift_two),
        sum_proj,
        sum_up,
    )
    attn_all = plus(attn_home[0], got_a0, got_attn)
    parts = [attn_all[0]] + [links.send(attn_all[k], links.far[k]) for k in range(1, count)]
    sums = sum_all(links, keep, away)
    layer_output = output_call(tie(place, sums, attn_all), middle, table, hidden, down_w)
    grad_attn = plus(*parts, kind=F32)

    d = layer_input.shape[1]
    heads = bias_qv.shape[1]
    vec = sums[0]
    total_out, total_down, gain_two, shift_two, gain_one, shift_one = (
        vec[i * d : (i + 1) * d] for i in range(6)
    )
    own = vec[6 * d :]
    total_qv = jnp.stack(
        [
            jnp.concatenate([own[0:128], own[384:448]]),
            jnp.concatenate([own[256:384], own[448:512]]),
        ]
    )
    total_up = own[640:]

    shard_qkv, shard_out = unpack_attn(grad_attn)
    return (
        layer_output,
        grad_input,
        shard_qkv,
        total_qv,
        shard_out,
        total_out,
        gain_one,
        shift_one,
        gain_two,
        shift_two,
        grad_up,
        total_up,
        grad_down.T,
        total_down,
    )


def solution(mesh):
    tokens = P(("fsdp", "tp"), None)
    placed = (
        tokens,
        P("fsdp", None, "tp"),
        P(None, "tp"),
        P("tp", "fsdp"),
        P(),
        P(),
        P(),
        P(),
        P(),
        P("fsdp", "tp"),
        P("tp"),
        P("tp", "fsdp"),
        P(),
        tokens,
    )
    return jax.shard_map(
        functools.partial(body, Links(mesh)),
        mesh=mesh,
        in_specs=placed,
        out_specs=(
            tokens,
            tokens,
            P("fsdp", None, "tp"),
            P(None, "tp"),
            P("tp", "fsdp"),
            P(),
            P(),
            P(),
            P(),
            P(),
            P("fsdp", "tp"),
            P("tp"),
            P("tp", "fsdp"),
            P(),
        ),
        check_vma=False,
    )
```

time: 532 us -> 317 us (0.60)
  Pallas kernels: 247 us -> 122 us
  waiting for transfers between devices: 138 us -> 77 us
  local copies, waits for them, and re-layouts: 71.4 us -> 40.1 us
  starting transfers between devices: 51.4 us -> 57.7 us
  other arithmetic: 17.7 us -> 11.8 us
    pallas_call x11 -> x17, Pallas kernels: 222 us -> 98.8 us  [the longest x4 36.2 us: attend_back_call(): pl.pallas_call(functools.partial(attend_back_kernel, count, len(gots)), g...]
    ppermute x59 -> x55, waiting for transfers between devices: 138 us -> 77 us  [send(): return lax.ppermute(value, AXES, pairs)]
    unnamed x203 -> x200, local copies, waits for them, and re-layouts: 49.9 us -> 37.4 us
    slice x27 -> x4, local copies, waits for them, and re-layouts: 8.26 us -> 0.76 us  [the longest x1 0.65 us: body(): vec[i * d:(i + 1) * d]]
    ppermute x59 -> x55, starting transfers between devices: 51.4 us -> 57.7 us  [send(): return lax.ppermute(value, AXES, pairs)]
    concatenate x9 -> x0, local copies, waits for them, and re-layouts: 6.02 us -> none  [the longest x4 1.6 us: body(): bias = jnp.concatenate([bq[:128], none, bv[:128], bq[128:], bv[128:], none])]
    reshape x14 -> x0, local copies, waits for them, and re-layouts: 5.48 us -> none  [body(): row = lambda v: v.reshape(1, -1)]
  transfers between devices with their start and end apart: 59 -> 55, of which waited for: 20 -> 18; matrix products, arithmetic and copies ran while one was open for 8% -> 4% of each run, Pallas kernels for 32% -> 39%
where the time goes in v2:
time: 317 us; the launch traced here: 311 us
  Pallas kernels  122 us (38%)
  waiting for transfers between devices  77 us (24%)
  starting transfers between devices  57.7 us (18%)
  local copies, waits for them, and re-layouts  40.1 us (13%)
  other arithmetic  11.8 us (4%)
    ppermute x55, waiting for transfers between devices, send(): return lax.ppermute(value, AXES, pairs)  77 us
    ppermute x55, starting transfers between devices, send(): return lax.ppermute(value, AXES, pairs)  57.7 us
    unnamed x200, local copies, waits for them, and re-layouts  37.4 us
    pallas_call x4, Pallas kernels, attend_back_call(): pl.pallas_call(functools.partial(attend_back_kernel, count, len(gots)), g...  36.2 us
    pallas_call x4, Pallas kernels, feed_call(): pl.pallas_call(functools.partial(feed_kernel, count, 512, len(gots)), gri...  33.2 us
    pallas_call x4, Pallas kernels, attend_call(): pl.pallas_call(attend_kernel, grid=(seqs,), in_specs=[pl.BlockSpec((SEQ_L...  18 us
    pallas_call x1, Pallas kernels, turn_call(): pl.pallas_call(turn_kernel, grid=(rows // tile,), in_specs=[pl.BlockSpec(...  9.47 us
    pallas_call x1, Pallas kernels, finish_call(): pl.pallas_call(finish_kernel, grid=(rows // tile,), in_specs=[pl.BlockSpe...  8.98 us
  transfers between devices with their start and end apart: 55, of which 18 were waited for; matrix products, arithmetic and copies ran while one was open for 4% of the time, Pallas kernels for 39%

profile of v2, /device:TPU:0, one launch (start us, length us, event | category | flops | bytes accessed | tf_op | source)
XLA Modules:
  0.0 310.7 jit_solution(11384411517850753059)
XLA Ops:
  0.6 3.0 collective-permute-start.1
  22.2 3.4 %collective-permute-done.5 = bf16[2,96,768]{2,1,0:T(8,128)(2,1)S(1)} collective-permute-done((bf16[2,96,768]{2,1,0:T(8,128)(2,1)S(1)}, bf16[2,96,768]{2,1,0:T(8,128)(2,1)S(1)}, u32[]{:S(2)}, u32[]{:S(2)}) %collective-permute-start.5) | collective-permute-done | bytes 294944 | tf_op jit(solution)/shard_map/ppermute | solution.py:632
  29.1 5.4 %collective-permute-done.6 = bf16[96,768]{1,0:T(8,128)(2,1)S(1)} collective-permute-done((bf16[96,768]{1,0:T(8,128)(2,1)S(1)}, bf16[96,768]{1,0:T(8,128)(2,1)S(1)}, u32[]{:S(2)}, u32[]{:S(2)}) %collective-permute-start.6) | collective-permute-done | bytes 147488 | tf_op jit(solution)/shard_map/ppermute | solution.py:632
  36.4 5.6 %collective-permute-done.7.refs_6_.refs_7_ = bf16[2,96,768]{2,1,0:T(8,128)(2,1)S(1)} collective-permute-done((bf16[2,96,768]{2,1,0:T(8,128)(2,1)S(1)}, bf16[2,96,768]{2,1,0:T(8,128)(2,1)S(1)}, u32[]{:S(2)}, u32[]{:S(2)}) %collective-permute-start.7) | collective-permute-done | bytes 294944 | tf_op jit(solution)/shard_map/ppermute | solution.py:632
  45.0 4.5 %attend.4 = (bf16[1024,640]{1,0:T(8,128)(2,1)S(1)}, bf16[1024,256]{1,0:T(8,128)(2,1)S(1)}, f32[2,8,512]{2,1,0:T(8,128)S(1)}) custom-call(bf16[1024,768]{1,0:T(8,128)(2,1)S(1)} %get-tuple-element.94.n1_ref, bf16[768,768]{1,0:T(8,128)(2,1)S(1)} %assemble.6.w_ref.refs_4_, f32[1,1536]{1,0:T(1,128)S(1)} %get-tuple-element.96.bias_ref.refs_2_), custom_call_target="tpu_custom_call" | custom-call | flops 1800000000 | bytes 2400000 | tf_op jit(solution)/shard_map/attend/pallas_call | solution.py:197
  50.9 8.0 %collective-permute-done.10.refs_0_.refs_1_.refs_4_.refs_5_ = bf16[2,2,96,768]{3,2,1,0:T(8,128)(2,1)S(1)} collective-permute-done((bf16[2,2,96,768]{3,2,1,0:T(8,128)(2,1)S(1)}, bf16[2,2,96,768]{3,2,1,0:T(8,128)(2,1)S(1)}, u32[]{:S(2)}, u32[]{:S(2)}) %collective-permute-start.10) | collective-permute-done | bytes 589856 | tf_op jit(solution)/shard_map/ppermute | solution.py:632
  61.1 4.5 %attend.5 = (bf16[1024,640]{1,0:T(8,128)(2,1)S(1)}, bf16[1024,256]{1,0:T(8,128)(2,1)S(1)}, f32[2,8,512]{2,1,0:T(8,128)S(1)}) custom-call(bf16[1024,768]{1,0:T(8,128)(2,1)S(1)} %get-tuple-element.94.n1_ref, bf16[768,768]{1,0:T(8,128)(2,1)S(1)} %collective-permute-done.8.w_ref.refs_5_, f32[1,1536]{1,0:T(1,128)S(1)} %collective-permute-done.9.bias_ref.refs_2_), custom_call_target="tpu_custom_call" | custom-call | flops 1800000000 | bytes 2400000 | tf_op jit(solution)/shard_map/attend/pallas_call | solution.py:197
  65.6 5.5 %collective-permute-done.11.refs_2_.refs_3_.refs_6_.refs_7_ = bf16[2,2,96,768]{3,2,1,0:T(8,128)(2,1)S(1)} collective-permute-done((bf16[2,2,96,768]{3,2,1,0:T(8,128)(2,1)S(1)}, bf16[2,2,96,768]{3,2,1,0:T(8,128)(2,1)S(1)}, u32[]{:S(2)}, u32[]{:S(2)}) %collective-permute-start.11) | collective-permute-done | bytes 589856 | tf_op jit(solution)/shard_map/ppermute | solution.py:632
  76.4 13.7 %collective-permute-done.19.refs_4_.refs_5_.refs_6_.refs_7_ = bf16[4,96,768]{2,1,0:T(8,128)(2,1)S(1)} collective-permute-done((bf16[4,96,768]{2,1,0:T(8,128)(2,1)S(1)}, bf16[4,96,768]{2,1,0:T(8,128)(2,1)S(1)}, u32[]{:S(2)}, u32[]{:S(2)}) %collective-permute-start.19) | collective-permute-done | bytes 589856 | tf_op jit(solution)/shard_map/ppermute | solution.py:632
  90.1 2.6 collective-permute-done.15.refs_2_.refs_6_
  95.2 4.5 %attend.6 = (bf16[1024,640]{1,0:T(8,128)(2,1)S(1)}, bf16[1024,256]{1,0:T(8,128)(2,1)S(1)}, f32[2,8,512]{2,1,0:T(8,128)S(1)}) custom-call(bf16[1024,768]{1,0:T(8,128)(2,1)S(1)} %copy-done.74, bf16[768,768]{1,0:T(8,128)(2,1)S(1)} %assemble.7.w_ref.refs_6_, f32[1,1536]{1,0:T(1,128)S(1)} %collective-permute-done.4.bias_ref.refs_2_), custom_call_target="tpu_custom_call" | custom-call | flops 1800000000 | bytes 2400000 | tf_op jit(solution)/shard_map/attend/pallas_call | solution.py:197
  99.8 4.5 %attend.7 = (bf16[1024,640]{1,0:T(8,128)(2,1)S(1)}, bf16[1024,256]{1,0:T(8,128)(2,1)S(1)}, f32[2,8,512]{2,1,0:T(8,128)S(1)}) custom-call(bf16[1024,768]{1,0:T(8,128)(2,1)S(1)} %copy-done.74, bf16[768,768]{1,0:T(8,128)(2,1)S(1)} %collective-permute-done.12.w_ref.refs_7_, f32[1,1536]{1,0:T(1,128)S(1)} %collective-permute-done.13.bias_ref.refs_2_), custom_call_target="tpu_custom_call" | custom-call | flops 1800000000 | bytes 2400000 | tf_op jit(solution)/shard_map/attend/pallas_call | solution.py:197
  105.6 3.6 %collective-permute-done.20.refs_3_.refs_7_ = bf16[2,2,96,768]{3,2,1,0:T(8,128)(2,1)S(1)} collective-permute-done((bf16[2,2,96,768]{3,2,1,0:T(8,128)(2,1)S(1)}, bf16[2,2,96,768]{3,2,1,0:T(8,128)(2,1)S(1)}, u32[]{:S(2)}, u32[]{:S(2)}) %collective-permute-start.20) | collective-permute-done | bytes 589856 | tf_op jit(solution)/shard_map/ppermute | solution.py:632
  109.9 10.2 %collective-permute-done.24.refs_0_.refs_1_.refs_2_.refs_3_ = bf16[4,96,768]{2,1,0:T(8,128)(2,1)S(1)} collective-permute-done((bf16[4,96,768]{2,1,0:T(8,128)(2,1)S(1)}, bf16[4,96,768]{2,1,0:T(8,128)(2,1)S(1)}, u32[]{:S(2)}, u32[]{:S(2)}) %collective-permute-start.24) | collective-permute-done | bytes 589856 | tf_op jit(solution)/shard_map/ppermute | solution.py:632
  122.2 3.5 %middle.1 = (f32[1024,768]{1,0:T(8,128)S(1)}, bf16[1024,768]{1,0:T(8,128)(2,1)S(1)}) custom-call(bf16[1024,768]{1,0:T(8,128)(2,1)S(1)} %copy-done.3, f32[8,768]{1,0:T(8,128)S(1)} %get-tuple-element.112.table_ref, bf16[1024,256]{1,0:T(8,128)(2,1)S(1)} %get-tuple-element.99.refs_0_.mixed_ref, bf16[1024,256]{1,0:T(8,128)(2,1)S(1)} %get-tuple-element.101.refs_1_.mixed_ref, ...), custom_call_target="tpu_custom_call" | custom-call | flops 483183808 | bytes 4800000 | tf_op jit(solution)/shard_map/middle/pallas_call | solution.py:237
  127.5 8.3 %feed.4 = (bf16[1024,768]{1,0:T(8,128)(2,1)S(1)}, bf16[1024,768]{1,0:T(8,128)(2,1)S(1)}, f32[1,768]{1,0:T(1,128)S(1)}, bf16[2,8,96,768]{3,2,1,0:T(8,128)(2,1)}) custom-call(s32[2]{0:T(128)S(1)} %pad_add_fusion.place_ref._, bf16[1024,768]{1,0:T(8,128)(2,1)S(1)} %get-tuple-element.113.n2_ref, bf16[1024,768]{1,0:T(8,128)(2,1)S(1)} %copy-done.1, ...), custom_call_target="tpu_custom_call" | custom-call | flops 1449551488 | bytes 4800000 | tf_op jit(solution)/shard_map/feed/pallas_call | solution.py:326
  137.0 8.3 %feed.6 = (bf16[1024,768]{1,0:T(8,128)(2,1)S(1)}, bf16[1024,768]{1,0:T(8,128)(2,1)S(1)}, f32[1,768]{1,0:T(1,128)S(1)}, bf16[2,8,96,768]{3,2,1,0:T(8,128)(2,1)}) custom-call(s32[2]{0:T(128)S(1)} %pad_add_fusion.place_ref._, bf16[1024,768]{1,0:T(8,128)(2,1)S(1)} %get-tuple-element.113.n2_ref, bf16[1024,768]{1,0:T(8,128)(2,1)S(1)} %copy-done.1, ...), custom_call_target="tpu_custom_call" | custom-call | flops 1449551488 | bytes 4800000 | tf_op jit(solution)/shard_map/feed/pallas_call | solution.py:326
  151.8 8.2 %feed.5 = (bf16[1024,768]{1,0:T(8,128)(2,1)S(1)}, bf16[1024,768]{1,0:T(8,128)(2,1)S(1)}, f32[1,768]{1,0:T(1,128)S(1)}, bf16[4,96,768]{2,1,0:T(8,128)(2,1)S(1)}, ...) custom-call(s32[2]{0:T(128)S(1)} %pad_add_fusion.place_ref._, ...), custom_call_target="tpu_custom_call" | custom-call | flops 1449551488 | bytes 4800000 | tf_op jit(solution)/shard_map/feed/pallas_call | solution.py:326
  163.2 8.5 %feed.7 = (bf16[1024,768]{1,0:T(8,128)(2,1)S(1)}, bf16[1024,768]{1,0:T(8,128)(2,1)S(1)}, f32[1,768]{1,0:T(1,128)S(1)}, bf16[4,96,768]{2,1,0:T(8,128)(2,1)S(1)}, ...) custom-call(s32[2]{0:T(128)S(1)} %pad_add_fusion.place_ref._, bf16[1024,768]{1,0:T(8,128)(2,1)S(1)} %get-tuple-element.113.n2_ref, ...), custom_call_target="tpu_custom_call" | custom-call | flops 1449551488 | bytes 4800000 | tf_op jit(solution)/shard_map/feed/pallas_call | solution.py:326
  179.8 9.5 %turn.1 = (f32[1024,768]{1,0:T(8,128)S(1)}, bf16[1024,768]{1,0:T(8,128)(2,1)S(1)}, f32[1,768]{1,0:T(1,128)S(1)}, f32[1,768]{1,0:T(1,128)S(1)}, f32[1,768]{1,0:T(1,128)S(1)}) custom-call(s32[2]{0:T(128)S(1)} %pad_add_fusion.place_ref._, f32[1024,768]{1,0:T(8,128)} %copy-done.4, bf16[1024,768]{1,0:T(8,128)(2,1)S(1)} %copy-done.1, f32[8,768]{1,0:T(8,128)S(1)} %copy-done.51, ...), custom_call_target="tpu_custom_call" | custom-call | flops 1449551488 | bytes 6000000 | tf_op jit(solution)/shard_map/turn/pallas_call | solution.py:371
  194.3 8.8 %attend_back.4 = (bf16[1024,640]{1,0:T(8,128)(2,1)S(1)}, f32[1,640]{1,0:T(1,128)S(1)}, bf16[8,96,768]{2,1,0:T(8,128)(2,1)S(1)}) custom-call(s32[2]{0:T(128)S(1)} %pad_add_fusion.place_ref._, bf16[1024,768]{1,0:T(8,128)(2,1)S(1)} %get-tuple-element.126.grows_ref, bf16[1024,768]{1,0:T(8,128)(2,1)S(1)} %copy-done.75, bf16[768,768]{1,0:T(8,128)(2,1)S(1)} %copy-done.9, ...), custom_call_target="tpu_custom_call" | custom-call | flops 3000000000 | bytes 3600000 | tf_op jit(solution)/shard_map/attend_back/pallas_call | solution.py:525
  207.5 9.0 %attend_back.6 = (bf16[1024,640]{1,0:T(8,128)(2,1)S(1)}, f32[1,640]{1,0:T(1,128)S(1)}, bf16[8,96,768]{2,1,0:T(8,128)(2,1)S(1)}) custom-call(s32[2]{0:T(128)S(1)} %pad_add_fusion.place_ref._, bf16[1024,768]{1,0:T(8,128)(2,1)S(1)} %copy-done.77, bf16[1024,768]{1,0:T(8,128)(2,1)S(1)} %copy-done.75, bf16[768,768]{1,0:T(8,128)(2,1)S(1)} %copy-done.7, ...), custom_call_target="tpu_custom_call" | custom-call | flops 3000000000 | bytes 3600000 | tf_op jit(solution)/shard_map/attend_back/pallas_call | solution.py:525
  222.0 9.1 %attend_back.5 = (bf16[1024,640]{1,0:T(8,128)(2,1)S(1)}, f32[1,640]{1,0:T(1,128)S(1)}, bf16[4,96,768]{2,1,0:T(8,128)(2,1)S(1)}, bf16[4,96,768]{2,1,0:T(8,128)(2,1)S(1)}) custom-call(s32[2]{0:T(128)S(1)} %pad_add_fusion.place_ref._, bf16[1024,768]{1,0:T(8,128)(2,1)S(1)} %copy-done.77, bf16[1024,768]{1,0:T(8,128)(2,1)S(1)} %copy-done.75, ...), custom_call_target="tpu_custom_call" | custom-call | flops 3000000000 | bytes 3600000 | tf_op jit(solution)/shard_map/attend_back/pallas_call | solution.py:525
  232.9 4.0 %collective-permute-start.50 = (bf16[96,768]{1,0:T(8,128)(2,1)}, bf16[96,768]{1,0:T(8,128)(2,1)}, u32[]{:S(2)}, u32[]{:S(2)}) collective-permute-start(bf16[96,768]{1,0:T(8,128)(2,1)} %get-tuple-element.200), channel_id=1, source_target_pairs={{0,16},{1,17},{2,18},{3,19},{4,20},{5,21},{6,22},{7,23},{8,24},{9,... | collective-permute-start | bytes 442376 | tf_op jit(solution)/shard_map/ppermute | solution.py:632
  237.0 9.3 %attend_back.7 = (bf16[1024,640]{1,0:T(8,128)(2,1)S(1)}, f32[1,640]{1,0:T(1,128)S(1)}, bf16[4,96,768]{2,1,0:T(8,128)(2,1)S(1)}, bf16[4,96,768]{2,1,0:T(8,128)(2,1)S(1)}) custom-call(s32[2]{0:T(128)S(1)} %pad_add_fusion.place_ref._, bf16[1024,768]{1,0:T(8,128)(2,1)S(1)} %copy-done.77, bf16[1024,768]{1,0:T(8,128)(2,1)S(1)} %copy-done.75, ...), custom_call_target="tpu_custom_call" | custom-call | flops 3000000000 | bytes 3600000 | tf_op jit(solution)/shard_map/attend_back/pallas_call | solution.py:525
  249.3 9.0 %finish.1 = (bf16[1024,768]{1,0:T(8,128)(2,1)}, f32[2,6016]{1,0:T(2,128)S(1)}, f32[2,6016]{1,0:T(2,128)S(1)}) custom-call(s32[2]{0:T(128)S(1)} %pad_add_fusion.place_ref._, bf16[1024,768]{1,0:T(8,128)(2,1)S(1)} %copy-done.3, f32[1024,768]{1,0:T(8,128)S(1)} %copy-done.18, f32[8,768]{1,0:T(8,128)S(1)} %copy-done.52, ...), custom_call_target="tpu_custom_call" | custom-call | flops 1207959552 | bytes 4800000 | tf_op jit(solution)/shard_map/finish/pallas_call | solution.py:577
  269.8 2.8 collective-permute-done.52
  272.5 5.1 %collective-permute-start.42 = (f32[1,6016]{1,0:T(1,128)S(1)}, f32[1,6016]{1,0:T(1,128)S(1)}, u32[]{:S(2)}, u32[]{:S(2)}) collective-permute-start(f32[1,6016]{1,0:T(1,128)S(1)} %add_add_fusion.1), channel_id=1, source_target_pairs={{0,16},{1,17},{2,18},{3,19},{4,20},{5,21},{6,22},{7,23},{8,24},{9,... | collective-permute-start | bytes 72200 | tf_op jit(solution)/shard_map/ppermute | solution.py:632
  277.8 4.5 %collective-permute-start.43 = (f32[1,6016]{1,0:T(1,128)S(1)}, f32[1,6016]{1,0:T(1,128)S(1)}, u32[]{:S(2)}, u32[]{:S(2)}) collective-permute-start(f32[1,6016]{1,0:T(1,128)S(1)} %add_add_fusion.1), channel_id=1, source_target_pairs={{0,24},{1,25},{2,26},{3,27},{4,28},{5,29},{6,30},{7,31},{8,16},{9,... | collective-permute-start | bytes 72200 | tf_op jit(solution)/shard_map/ppermute | solution.py:632
  285.3 11.0 %collective-permute-done.45 = bf16[4,96,768]{2,1,0:T(8,128)(2,1)S(1)} collective-permute-done((bf16[4,96,768]{2,1,0:T(8,128)(2,1)S(1)}, bf16[4,96,768]{2,1,0:T(8,128)(2,1)S(1)}, u32[]{:S(2)}, u32[]{:S(2)}) %collective-permute-start.45) | collective-permute-done | bytes 589856 | tf_op jit(solution)/shard_map/ppermute | solution.py:632
  298.2 2.3 collective-permute-start.48
  301.1 7.2 %output.1 = bf16[1024,768]{1,0:T(8,128)(2,1)} custom-call(s32[2]{0:T(128)S(1)} %pad_add_fusion.place_ref._, f32[1024,768]{1,0:T(8,128)S(1)} %copy-done.5, f32[8,768]{1,0:T(8,128)S(1)} %copy-done.52, bf16[1024,768]{1,0:T(8,128)(2,1)S(1)} %copy-done.26, bf16[1024,768]{1,0:T(8,128)(2,1)S(1)} %copy-done.22, bf16[1024,768]{1,0:T(8,128)(2,1)S(1)} %copy-done.28, ...), custom_call_target="tpu_custom_call" | custom-call | flops 1449551488 | bytes 4800000 | tf_op jit(solution)/shard_map/output/pallas_call | solution.py:405
  (346 shorter events, 101.5 us)
Async XLA Ops:
  0.6 16.6 %collective-permute-start.1 = (bf16[96,768]{1,0:T(8,128)(2,1)}, bf16[96,768]{1,0:T(8,128)(2,1)S(1)}, u32[]{:S(2)}, u32[]{:S(2)}) collective-permute-start(bf16[96,768]{1,0:T(8,128)(2,1)} %param.23), channel_id=1, source_target_pairs={{0,4},{1,5},{2,6},{3,7},{4,0},{5,1},{6,2},{7,3},{8,12},{9,13},{10,... | collective-permute-start | bytes 442376 | tf_op jit(solution)/shard_map/ppermute | solution.py:632
  42.6 17.1 %collective-permute-start.8 = (bf16[768,768]{1,0:T(8,128)(2,1)S(1)}, bf16[768,768]{1,0:T(8,128)(2,1)S(1)}, u32[]{:S(2)}, u32[]{:S(2)}) collective-permute-start(bf16[768,768]{1,0:T(8,128)(2,1)S(1)} %assemble.6.w_ref.refs_4_), channel_id=1, source_target_pairs={{0,1},{1,0},{2,3},{3,2},{4,5},{5,4},{6,7},{7,6},{8,9},{9,8},{10,11... | collective-permute-start | bytes 3538952 | tf_op jit(solution)/shard_map/ppermute | solution.py:632
  42.7 16.2 %collective-permute-start.10 = (bf16[2,2,96,768]{3,2,1,0:T(8,128)(2,1)S(1)}, bf16[2,2,96,768]{3,2,1,0:T(8,128)(2,1)S(1)}, u32[]{:S(2)}, u32[]{:S(2)}) collective-permute-start(bf16[2,2,96,768]{3,2,1,0:T(8,128)(2,1)S(1)} %pad_maximum_fusion.1), channel_id=1, source_target_pairs={{0,2},{1,3},{2,0},{3,1},{4,6},{5,7},{6,4},{7,5},{8,10},{9,11},{10,... | collective-permute-start | bytes 1769480 | tf_op jit(solution)/shard_map/ppermute | solution.py:632
  43.6 27.6 %collective-permute-start.11 = (bf16[2,2,96,768]{3,2,1,0:T(8,128)(2,1)S(1)}, bf16[2,2,96,768]{3,2,1,0:T(8,128)(2,1)S(1)}, u32[]{:S(2)}, u32[]{:S(2)}) collective-permute-start(bf16[2,2,96,768]{3,2,1,0:T(8,128)(2,1)S(1)} %pad_maximum_fusion.2), channel_id=1, source_target_pairs={{0,2},{1,3},{2,0},{3,1},{4,6},{5,7},{6,4},{7,5},{8,10},{9,11},{10,... | collective-permute-start | bytes 1769480 | tf_op jit(solution)/shard_map/ppermute | solution.py:632
  45.0 30.8 %collective-permute-start.14 = (bf16[2,2,96,768]{3,2,1,0:T(8,128)(2,1)S(1)}, bf16[2,2,96,768]{3,2,1,0:T(8,128)(2,1)S(1)}, u32[]{:S(2)}, u32[]{:S(2)}) collective-permute-start(bf16[2,2,96,768]{3,2,1,0:T(8,128)(2,1)S(1)} %pad_maximum_fusion.refs_0_.refs_4_), channel_id=1, source_target_pairs={{0,8},{1,9},{2,10},{3,11},{4,12},{5,13},{6,14},{7,15},{8,16},{9,17... | collective-permute-start | bytes 1769480 | tf_op jit(solution)/shard_map/ppermute | solution.py:632
  49.5 22.4 %collective-permute-start.16 = (bf16[96,768]{1,0:T(8,128)(2,1)S(1)}, bf16[96,768]{1,0:T(8,128)(2,1)S(1)}, u32[]{:S(2)}, u32[]{:S(2)}) collective-permute-start(bf16[96,768]{1,0:T(8,128)(2,1)S(1)} %bitcast.89), channel_id=1, source_target_pairs={{0,8},{1,9},{2,10},{3,11},{4,12},{5,13},{6,14},{7,15},{8,16},{9,17... | collective-permute-start | bytes 442376 | tf_op jit(solution)/shard_map/ppermute | solution.py:632
  58.9 13.5 %collective-permute-start.17 = (bf16[96,768]{1,0:T(8,128)(2,1)S(1)}, bf16[96,768]{1,0:T(8,128)(2,1)S(1)}, u32[]{:S(2)}, u32[]{:S(2)}) collective-permute-start(bf16[96,768]{1,0:T(8,128)(2,1)S(1)} %bitcast.90), channel_id=1, source_target_pairs={{0,16},{1,17},{2,18},{3,19},{4,20},{5,21},{6,22},{7,23},{8,24},{9,... | collective-permute-start | bytes 442376 | tf_op jit(solution)/shard_map/ppermute | solution.py:632
  71.8 28.0 %collective-permute-start.12 = (bf16[768,768]{1,0:T(8,128)(2,1)S(1)}, bf16[768,768]{1,0:T(8,128)(2,1)S(1)}, u32[]{:S(2)}, u32[]{:S(2)}) collective-permute-start(bf16[768,768]{1,0:T(8,128)(2,1)S(1)} %assemble.7.w_ref.refs_6_), channel_id=1, source_target_pairs={{0,1},{1,0},{2,3},{3,2},{4,5},{5,4},{6,7},{7,6},{8,9},{9,8},{10,11... | collective-permute-start | bytes 3538952 | tf_op jit(solution)/shard_map/ppermute | solution.py:632
  74.7 15.4 %collective-permute-start.19 = (bf16[4,96,768]{2,1,0:T(8,128)(2,1)S(1)}, bf16[4,96,768]{2,1,0:T(8,128)(2,1)S(1)}, u32[]{:S(2)}, u32[]{:S(2)}) collective-permute-start(bf16[4,96,768]{2,1,0:T(8,128)(2,1)S(1)} %pad_maximum_fusion.3.refs_0_.refs_1_.refs_2_.refs_3_), channel_id=1, source_target_pairs={{0,4},{1,5},{2,6},{3,7},{4,0},{5,1},{6,2},{7,3},{8,12},{9,13},{10,... | collective-permute-start | bytes 1769480 | tf_op jit(solution)/shard_map/ppermute | solution.py:632
  75.8 16.9 %collective-permute-start.15 = (bf16[2,2,96,768]{3,2,1,0:T(8,128)(2,1)S(1)}, bf16[2,2,96,768]{3,2,1,0:T(8,128)(2,1)S(1)}, u32[]{:S(2)}, u32[]{:S(2)}) collective-permute-start(bf16[2,2,96,768]{3,2,1,0:T(8,128)(2,1)S(1)} %collective-permute-done.14.refs_1_.refs_5_), channel_id=1, source_target_pairs={{0,8},{1,9},{2,10},{3,11},{4,12},{5,13},{6,14},{7,15},{8,16},{9,17... | collective-permute-start | bytes 1769480 | tf_op jit(solution)/shard_map/ppermute | solution.py:632
  92.7 16.5 %collective-permute-start.20 = (bf16[2,2,96,768]{3,2,1,0:T(8,128)(2,1)S(1)}, bf16[2,2,96,768]{3,2,1,0:T(8,128)(2,1)S(1)}, u32[]{:S(2)}, u32[]{:S(2)}) collective-permute-start(bf16[2,2,96,768]{3,2,1,0:T(8,128)(2,1)S(1)} %collective-permute-done.15.refs_2_.refs_6_), channel_id=1, source_target_pairs={{0,8},{1,9},{2,10},{3,11},{4,12},{5,13},{6,14},{7,15},{8,16},{9,17... | collective-permute-start | bytes 1769480 | tf_op jit(solution)/shard_map/ppermute | solution.py:632
  93.2 16.7 %collective-permute-start.25 = (bf16[4,96,768]{2,1,0:T(8,128)(2,1)S(1)}, bf16[4,96,768]{2,1,0:T(8,128)(2,1)S(1)}, u32[]{:S(2)}, u32[]{:S(2)}) collective-permute-start(bf16[4,96,768]{2,1,0:T(8,128)(2,1)S(1)} %collective-permute-done.19.refs_4_.refs_5_.refs_6_.refs_7_), channel_id=1, source_target_pairs={{0,2},{1,3},{2,0},{3,1},{4,6},{5,7},{6,4},{7,5},{8,10},{9,11},{10,... | collective-permute-start | bytes 1769480 | tf_op jit(solution)/shard_map/ppermute | solution.py:632
  93.7 26.4 %collective-permute-start.24 = (bf16[4,96,768]{2,1,0:T(8,128)(2,1)S(1)}, bf16[4,96,768]{2,1,0:T(8,128)(2,1)S(1)}, u32[]{:S(2)}, u32[]{:S(2)}) collective-permute-start(bf16[4,96,768]{2,1,0:T(8,128)(2,1)S(1)} %pad_maximum_fusion.3.refs_0_.refs_1_.refs_2_.refs_3_), channel_id=1, source_target_pairs={{0,2},{1,3},{2,0},{3,1},{4,6},{5,7},{6,4},{7,5},{8,10},{9,11},{10,... | collective-permute-start | bytes 1769480 | tf_op jit(solution)/shard_map/ppermute | solution.py:632
  105.6 21.9 %collective-permute-start.22 = (bf16[768,768]{1,0:T(8,128)(2,1)S(1)}, bf16[768,768]{1,0:T(8,128)(2,1)S(1)}, u32[]{:S(2)}, u32[]{:S(2)}) collective-permute-start(bf16[768,768]{1,0:T(8,128)(2,1)S(1)} %assemble.10.refs_1_.refs_4_), channel_id=1, source_target_pairs={{0,1},{1,0},{2,3},{3,2},{4,5},{5,4},{6,7},{7,6},{8,9},{9,8},{10,11... | collective-permute-start | bytes 3538952 | tf_op jit(solution)/shard_map/ppermute | solution.py:632
  109.8 17.7 %collective-permute-start.21 = (bf16[768,768]{1,0:T(8,128)(2,1)S(1)}, bf16[768,768]{1,0:T(8,128)(2,1)S(1)}, u32[]{:S(2)}, u32[]{:S(2)}) collective-permute-start(bf16[768,768]{1,0:T(8,128)(2,1)S(1)} %assemble.8.refs_0_.refs_4_), channel_id=1, source_target_pairs={{0,1},{1,0},{2,3},{3,2},{4,5},{5,4},{6,7},{7,6},{8,9},{9,8},{10,11... | collective-permute-start | bytes 3538952 | tf_op jit(solution)/shard_map/ppermute | solution.py:632
  120.7 16.2 %collective-permute-start.27 = (bf16[768,768]{1,0:T(8,128)(2,1)S(1)}, bf16[768,768]{1,0:T(8,128)(2,1)S(1)}, u32[]{:S(2)}, u32[]{:S(2)}) collective-permute-start(bf16[768,768]{1,0:T(8,128)(2,1)S(1)} %assemble.11.refs_1_.refs_6_), channel_id=1, source_target_pairs={{0,1},{1,0},{2,3},{3,2},{4,5},{5,4},{6,7},{7,6},{8,9},{9,8},{10,11... | collective-permute-start | bytes 3538952 | tf_op jit(solution)/shard_map/ppermute | solution.py:632
  121.5 15.5 %collective-permute-start.26 = (bf16[768,768]{1,0:T(8,128)(2,1)S(1)}, bf16[768,768]{1,0:T(8,128)(2,1)S(1)}, u32[]{:S(2)}, u32[]{:S(2)}) collective-permute-start(bf16[768,768]{1,0:T(8,128)(2,1)S(1)} %assemble.9.refs_0_.refs_6_), channel_id=1, source_target_pairs={{0,1},{1,0},{2,3},{3,2},{4,5},{5,4},{6,7},{7,6},{8,9},{9,8},{10,11... | collective-permute-start | bytes 3538952 | tf_op jit(solution)/shard_map/ppermute | solution.py:632
  148.3 15.0 %collective-permute-start.28 = (bf16[2,8,96,768]{3,2,1,0:T(8,128)(2,1)}, bf16[2,8,96,768]{3,2,1,0:T(8,128)(2,1)S(1)}, u32[]{:S(2)}, u32[]{:S(2)}) collective-permute-start(bf16[2,8,96,768]{3,2,1,0:T(8,128)(2,1)} %get-tuple-element.118), channel_id=1, source_target_pairs={{0,1},{1,0},{2,3},{3,2},{4,5},{5,4},{6,7},{7,6},{8,9},{9,8},{10,11... | collective-permute-start | bytes 7077896 | tf_op jit(solution)/shard_map/ppermute | solution.py:632
  162.2 28.9 %collective-permute-start.30 = (bf16[4,96,768]{2,1,0:T(8,128)(2,1)}, bf16[4,96,768]{2,1,0:T(8,128)(2,1)}, u32[]{:S(2)}, u32[]{:S(2)}) collective-permute-start(bf16[4,96,768]{2,1,0:T(8,128)(2,1)} %get-tuple-element.129), channel_id=1, source_target_pairs={{0,4},{1,5},{2,6},{3,7},{4,0},{5,1},{6,2},{7,3},{8,12},{9,13},{10,... | collective-permute-start | bytes 1769480 | tf_op jit(solution)/shard_map/ppermute | solution.py:632
  174.0 30.3 %collective-permute-start.34 = (bf16[4,96,768]{2,1,0:T(8,128)(2,1)}, bf16[4,96,768]{2,1,0:T(8,128)(2,1)S(1)}, u32[]{:S(2)}, u32[]{:S(2)}) collective-permute-start(bf16[4,96,768]{2,1,0:T(8,128)(2,1)} %get-tuple-element.140), channel_id=1, source_target_pairs={{0,4},{1,5},{2,6},{3,7},{4,0},{5,1},{6,2},{7,3},{8,12},{9,13},{10,... | collective-permute-start | bytes 1769480 | tf_op jit(solution)/shard_map/ppermute | solution.py:632
  175.1 41.7 %collective-permute-start.29 = (bf16[8,96,768]{2,1,0:T(8,128)(2,1)}, bf16[8,96,768]{2,1,0:T(8,128)(2,1)}, u32[]{:S(2)}, u32[]{:S(2)}) collective-permute-start(bf16[8,96,768]{2,1,0:T(8,128)(2,1)} %get-tuple-element.119), channel_id=1, source_target_pairs={{0,2},{1,3},{2,0},{3,1},{4,6},{5,7},{6,4},{7,5},{8,10},{9,11},{10,... | collective-permute-start | bytes 3538952 | tf_op jit(solution)/shard_map/ppermute | solution.py:632
  204.3 17.4 %collective-permute-start.31 = (bf16[8,96,768]{2,1,0:T(8,128)(2,1)S(1)}, bf16[8,96,768]{2,1,0:T(8,128)(2,1)S(1)}, u32[]{:S(2)}, u32[]{:S(2)}) collective-permute-start(bf16[8,96,768]{2,1,0:T(8,128)(2,1)S(1)} %get-tuple-element.133), channel_id=1, source_target_pairs={{0,1},{1,0},{2,3},{3,2},{4,5},{5,4},{6,7},{7,6},{8,9},{9,8},{10,11... | collective-permute-start | bytes 3538952 | tf_op jit(solution)/shard_map/ppermute | solution.py:632
  204.5 15.8 %collective-permute-start.35 = (bf16[4,96,768]{2,1,0:T(8,128)(2,1)S(1)}, bf16[4,96,768]{2,1,0:T(8,128)(2,1)S(1)}, u32[]{:S(2)}, u32[]{:S(2)}) collective-permute-start(bf16[4,96,768]{2,1,0:T(8,128)(2,1)S(1)} %add_convert_fusion.2), channel_id=1, source_target_pairs={{0,2},{1,3},{2,0},{3,1},{4,6},{5,7},{6,4},{7,5},{8,10},{9,11},{10,... | collective-permute-start | bytes 1769480 | tf_op jit(solution)/shard_map/ppermute | solution.py:632
  216.6 20.4 %collective-permute-start.36 = (bf16[8,96,768]{2,1,0:T(8,128)(2,1)S(1)}, bf16[8,96,768]{2,1,0:T(8,128)(2,1)S(1)}, u32[]{:S(2)}, u32[]{:S(2)}) collective-permute-start(bf16[8,96,768]{2,1,0:T(8,128)(2,1)S(1)} %get-tuple-element.148), channel_id=1, source_target_pairs={{0,1},{1,0},{2,3},{3,2},{4,5},{5,4},{6,7},{7,6},{8,9},{9,8},{10,11... | collective-permute-start | bytes 3538952 | tf_op jit(solution)/shard_map/ppermute | solution.py:632
  219.0 27.3 %collective-permute-start.33 = (bf16[4,96,768]{2,1,0:T(8,128)(2,1)}, bf16[4,96,768]{2,1,0:T(8,128)(2,1)}, u32[]{:S(2)}, u32[]{:S(2)}) collective-permute-start(bf16[4,96,768]{2,1,0:T(8,128)(2,1)} %add_convert_fusion.5), channel_id=1, source_target_pairs={{0,4},{1,5},{2,6},{3,7},{4,0},{5,1},{6,2},{7,3},{8,12},{9,13},{10,... | collective-permute-start | bytes 1769480 | tf_op jit(solution)/shard_map/ppermute | solution.py:632
  231.1 16.9 %collective-permute-start.32 = (bf16[4,96,768]{2,1,0:T(8,128)(2,1)S(1)}, bf16[4,96,768]{2,1,0:T(8,128)(2,1)S(1)}, u32[]{:S(2)}, u32[]{:S(2)}) collective-permute-start(bf16[4,96,768]{2,1,0:T(8,128)(2,1)S(1)} %get-tuple-element.135), channel_id=1, source_target_pairs={{0,4},{1,5},{2,6},{3,7},{4,0},{5,1},{6,2},{7,3},{8,12},{9,13},{10,... | collective-permute-start | bytes 1769480 | tf_op jit(solution)/shard_map/ppermute | solution.py:632
  232.9 25.4 %collective-permute-start.49 = (bf16[96,768]{1,0:T(8,128)(2,1)}, bf16[96,768]{1,0:T(8,128)(2,1)S(1)}, u32[]{:S(2)}, u32[]{:S(2)}) collective-permute-start(bf16[96,768]{1,0:T(8,128)(2,1)} %get-tuple-element.198), channel_id=1, source_target_pairs={{0,8},{1,9},{2,10},{3,11},{4,12},{5,13},{6,14},{7,15},{8,16},{9,17... | collective-permute-start | bytes 442376 | tf_op jit(solution)/shard_map/ppermute | solution.py:632
  232.9 25.4 %collective-permute-start.50 = (bf16[96,768]{1,0:T(8,128)(2,1)}, bf16[96,768]{1,0:T(8,128)(2,1)}, u32[]{:S(2)}, u32[]{:S(2)}) collective-permute-start(bf16[96,768]{1,0:T(8,128)(2,1)} %get-tuple-element.200), channel_id=1, source_target_pairs={{0,16},{1,17},{2,18},{3,19},{4,20},{5,21},{6,22},{7,23},{8,24},{9,... | collective-permute-start | bytes 442376 | tf_op jit(solution)/shard_map/ppermute | solution.py:632
  237.0 21.3 %collective-permute-start.51 = (bf16[96,768]{1,0:T(8,128)(2,1)S(1)}, bf16[96,768]{1,0:T(8,128)(2,1)}, u32[]{:S(2)}, u32[]{:S(2)}) collective-permute-start(bf16[96,768]{1,0:T(8,128)(2,1)S(1)} %get-tuple-element.199), channel_id=1, source_target_pairs={{0,24},{1,25},{2,26},{3,27},{4,28},{5,29},{6,30},{7,31},{8,0},{9,1... | collective-permute-start | bytes 442376 | tf_op jit(solution)/shard_map/ppermute | solution.py:632
  266.5 15.7 %collective-permute-start.54 = (bf16[96,768]{1,0:T(8,128)(2,1)S(1)}, bf16[96,768]{1,0:T(8,128)(2,1)S(1)}, u32[]{:S(2)}, u32[]{:S(2)}) collective-permute-start(bf16[96,768]{1,0:T(8,128)(2,1)S(1)} %get-tuple-element.196), channel_id=1, source_target_pairs={{0,24},{1,25},{2,26},{3,27},{4,28},{5,29},{6,30},{7,31},{8,0},{9,1... | collective-permute-start | bytes 442376 | tf_op jit(solution)/shard_map/ppermute | solution.py:632
  268.6 16.7 %collective-permute-start.44 = (bf16[4,96,768]{2,1,0:T(8,128)(2,1)S(1)}, bf16[4,96,768]{2,1,0:T(8,128)(2,1)S(1)}, u32[]{:S(2)}, u32[]{:S(2)}) collective-permute-start(bf16[4,96,768]{2,1,0:T(8,128)(2,1)S(1)} %get-tuple-element.167), channel_id=1, source_target_pairs={{0,4},{1,5},{2,6},{3,7},{4,0},{5,1},{6,2},{7,3},{8,12},{9,13},{10,... | collective-permute-start | bytes 1769480 | tf_op jit(solution)/shard_map/ppermute | solution.py:632
  269.6 14.8 %collective-permute-start.41 = (f32[1,6016]{1,0:T(1,128)S(1)}, f32[1,6016]{1,0:T(1,128)S(1)}, u32[]{:S(2)}, u32[]{:S(2)}) collective-permute-start(f32[1,6016]{1,0:T(1,128)S(1)} %add_add_fusion.1), channel_id=1, source_target_pairs={{0,8},{1,9},{2,10},{3,11},{4,12},{5,13},{6,14},{7,15},{8,0},{9,1},... | collective-permute-start | bytes 72200 | tf_op jit(solution)/shard_map/ppermute | solution.py:632
  (122 other events, 1346.8 us)
